TPU v7x, 32 devices: a whole 2x2x4 slice. The times are simulated.
32 devices in a mesh: section: 2 (over core), seq: 4 (over y, x), fsdp: 4 (over z).
Axes of the slice: x: 2, y: 2, z: 4, core: 2. Of those that a mesh axis runs over, the one named last changes fastest.
Arguments:
- inputs: bfloat16 [2, 1024, 1024], P(None, ('seq', 'fsdp')), may hold values from -6 to 6
- cotangent: bfloat16 [2, 1024, 1024], P(None, ('seq', 'fsdp')), may hold values from -6 to 6
- segment_ids: int32 [2, 1024], replicated, may hold values from 0 to 22, as said below
- ln1_gain: bfloat16 [2, 1024], P('section', 'fsdp'), may hold values from 0.5 to 1.5
- ln1_bias: bfloat16 [2, 1024], P('section', 'fsdp'), may hold values from -1 to 1
- w_qkv: bfloat16 [2, 1024, 3072], P('section', 'fsdp'), may hold values from -0.25 to 0.25
- b_query: bfloat16 [2, 1024], P('section', 'fsdp'), may hold values from -1.5 to 1.5
- b_value: bfloat16 [2, 1024], P('section', 'fsdp'), may hold values from -1.5 to 1.5
- w_out: bfloat16 [2, 1024, 1024], P('section', 'fsdp'), may hold values from -0.75 to 0.75
- b_out: bfloat16 [2, 1024], P('section', 'fsdp'), may hold values from -1.5 to 1.5
- ln2_gain: bfloat16 [2, 1024], P('section', 'fsdp'), may hold values from 0.5 to 1.5
- ln2_bias: bfloat16 [2, 1024], P('section', 'fsdp'), may hold values from -1 to 1
- w_fc: bfloat16 [2, 1024, 4096], P('section', 'fsdp'), may hold values from -0.1875 to 0.1875
- b_fc: bfloat16 [2, 4096], P('section', 'fsdp'), may hold values from -1.5 to 1.5
- w_proj: bfloat16 [2, 4096, 1024], P('section', 'fsdp'), may hold values from -0.125 to 0.125
- b_proj: bfloat16 [2, 1024], P('section', 'fsdp'), may hold values from -1.5 to 1.5
Outputs:
- relay_ends: float32 [2, 2, 1024, 1024], P('section', None, ('seq', 'fsdp'))
- grad_ln1_gain: float32 [2, 1024], P('section', ('seq', 'fsdp'))
- grad_ln1_bias: float32 [2, 1024], P('section', ('seq', 'fsdp'))
- grad_w_qkv: float32 [2, 1024, 3072], P('section', ('seq', 'fsdp'))
- grad_b_query: float32 [2, 1024], P('section', ('seq', 'fsdp'))
- grad_b_value: float32 [2, 1024], P('section', ('seq', 'fsdp'))
- grad_w_out: float32 [2, 1024, 1024], P('section', ('seq', 'fsdp'))
- grad_b_out: float32 [2, 1024], P('section', ('seq', 'fsdp'))
- grad_ln2_gain: float32 [2, 1024], P('section', ('seq', 'fsdp'))
- grad_ln2_bias: float32 [2, 1024], P('section', ('seq', 'fsdp'))
- grad_w_fc: float32 [2, 1024, 4096], P('section', ('seq', 'fsdp'))
- grad_b_fc: float32 [2, 4096], P('section', ('seq', 'fsdp'))
- grad_w_proj: float32 [2, 4096, 1024], P('section', ('seq', 'fsdp'))
- grad_b_proj: float32 [2, 1024], P('section', ('seq', 'fsdp'))
Inputs may be any that keep to these rules, and one draw needn't show every extreme that they name: `segment_ids`: each row numbers its documents in order of position, the first 22 and each next one less; every document has 51 to 512 tokens and in every row the first or the second has exactly 512; the tokens after the row's last whole document are padding, numbered 0.
All inputs are finite; a program needn't handle non-finite values.
Results may differ from a plain program's by a relative error of at most 0.024.
Values may be sent and summed in bfloat16 or wider, within the bound.
No kernel may reach another device: no remote copies, remote signals or barrier semaphores. Data moves between devices by JAX's collectives and lax.ppermute only.
A program may use at most 192 MiB of HBM per device.

v0:
```python
import math

import jax
import jax.numpy as jnp
from jax import lax
from jax.sharding import PartitionSpec as P

DH = 64


EPSILON = 1e-05
NEGATIVE = -1e30


def shifted(block, axis, distance):
    devices = range(lax.axis_size(axis))
    route = [(i - distance, i) for i in devices if i - distance in devices]
    return lax.ppermute(block, axis, route)


def layer_norm(values, gain_vec, bias_vec):
    average = jnp.mean(values, axis=-1, keepdims=True)
    centred = values - average
    variance = jnp.mean(centred * centred, axis=-1, keepdims=True)
    return centred * lax.rsqrt(variance + EPSILON) * gain_vec + bias_vec


def gelu_tanh(values):
    return jax.nn.gelu(values, approximate=True)


def mask_rows(seg_row, fsdp_index, n_seq, n_fsdp, tok_rows):
    places = jnp.arange(seg_row.shape[0], dtype=jnp.int32)
    seg_grid = seg_row.reshape(n_seq, n_fsdp, tok_rows)
    place_grid = places.reshape(n_seq, n_fsdp, tok_rows)
    query_ids = lax.dynamic_index_in_dim(seg_grid, fsdp_index, 1, keepdims=False).reshape(-1)
    query_places = lax.dynamic_index_in_dim(place_grid, fsdp_index, 1, keepdims=False).reshape(-1)
    key_ids = jnp.transpose(seg_grid, (1, 0, 2)).reshape(-1)
    key_places = jnp.transpose(place_grid, (1, 0, 2)).reshape(-1)
    same_doc = (query_ids[:, None] == key_ids[None, :]) & (query_ids[:, None] > 0)
    itself = query_places[:, None] == key_places[None, :]
    return (key_places[None, :] <= query_places[:, None]) & (same_doc | itself)


def split_heads(matrix):
    return matrix.reshape(matrix.shape[0], matrix.shape[1] // DH, DH)


def block_rows(matrix, block_len):
    return matrix.reshape((matrix.shape[0] // block_len, block_len) + matrix.shape[1:])


def masked_scores(queries, key_rows, allowed):
    raw_scores = jnp.einsum(
        "qhd,khd->hqk",
        split_heads(queries),
        split_heads(key_rows),
        preferred_element_type=jnp.float32,
    )
    return jnp.where(allowed[None], raw_scores * DH ** (-0.5), NEGATIVE)


def body(
    inputs,
    cotangent,
    segment_ids,
    ln1_gain,
    ln1_bias,
    w_qkv,
    b_query,
    b_value,
    w_out,
    b_out,
    ln2_gain,
    ln2_bias,
    w_fc,
    b_fc,
    w_proj,
    b_proj,
):
    n_seq = lax.axis_size("seq")
    n_fsdp = lax.axis_size("fsdp")
    section_index = lax.axis_index("section")
    fsdp_index = lax.axis_index("fsdp")
    last_section = section_index == 1
    micro, tok_rows, width = inputs.shape
    score_scale = DH ** (-0.5)
    query_count = tok_rows * n_seq
    block_len = math.gcd(query_count, 512)

    def fetch_params():
        return (
            lax.all_gather(ln1_gain[0], "fsdp", axis=0, tiled=True),
            lax.all_gather(ln1_bias[0], "fsdp", axis=0, tiled=True),
            lax.all_gather(w_qkv[0], "fsdp", axis=0, tiled=True),
            lax.all_gather(b_query[0], "fsdp", axis=0, tiled=True),
            lax.all_gather(b_value[0], "fsdp", axis=0, tiled=True),
            lax.all_gather(w_out[0], "fsdp", axis=0, tiled=True),
            lax.all_gather(b_out[0], "fsdp", axis=0, tiled=True),
            lax.all_gather(ln2_gain[0], "fsdp", axis=0, tiled=True),
            lax.all_gather(ln2_bias[0], "fsdp", axis=0, tiled=True),
            lax.all_gather(w_fc[0], "fsdp", axis=0, tiled=True),
            lax.all_gather(b_fc[0], "fsdp", axis=0, tiled=True),
            lax.all_gather(w_proj[0], "fsdp", axis=0, tiled=True),
            lax.all_gather(b_proj[0], "fsdp", axis=0, tiled=True),
        )

    received = jnp.zeros((tok_rows, width), jnp.bfloat16)
    kept_ticks = []
    layer_outs = []
    for tick_index in range(micro + 1):
        params = fetch_params()
        batch_index = jnp.clip(tick_index - section_index, 0, micro - 1)
        seg_row = lax.dynamic_index_in_dim(segment_ids, batch_index, 0, keepdims=False)
        allowed = mask_rows(seg_row, fsdp_index, n_seq, n_fsdp, tok_rows)
        if tick_index < micro:
            first_in = inputs[tick_index].astype(jnp.float32)
        else:
            first_in = jnp.zeros((tok_rows, width), jnp.float32)
        layer_in = jnp.where(last_section, received.astype(jnp.float32), first_in)
        (
            forward_gain_one,
            forward_bias_one,
            forward_w_mixed,
            forward_bias_query,
            forward_bias_value,
            forward_w_output,
            forward_bias_output,
            forward_gain_two,
            forward_bias_two,
            forward_w_hidden,
            forward_bias_hidden,
            forward_w_back,
            forward_bias_back,
        ) = params
        forward_normed = layer_norm(
            layer_in, forward_gain_one.astype(jnp.float32), forward_bias_one.astype(jnp.float32)
        ).astype(jnp.bfloat16)
        mixed_proj = jnp.dot(forward_normed, forward_w_mixed, preferred_element_type=jnp.float32)
        bias_row = jnp.concatenate(
            [forward_bias_query, jnp.zeros_like(forward_bias_query), forward_bias_value]
        ).astype(jnp.float32)
        mixed_tok = (mixed_proj + bias_row).astype(jnp.bfloat16).reshape(tok_rows, 3, width)
        head_rows = lax.all_to_all(mixed_tok, "seq", split_axis=2, concat_axis=0, tiled=True)
        forward_queries = head_rows[:, 0]
        forward_key_rows = lax.all_gather(head_rows[:, 1], "fsdp", axis=0, tiled=True)
        forward_value_rows = lax.all_gather(head_rows[:, 2], "fsdp", axis=0, tiled=True)

        def attend_block(operands):
            query_block, allowed_block = operands
            scores = masked_scores(query_block, forward_key_rows, allowed_block)
            row_top = jnp.max(scores, axis=-1, keepdims=True)
            log_block = row_top + jnp.log(
                jnp.sum(jnp.exp(scores - row_top), axis=-1, keepdims=True)
            )
            attn_weights = jnp.exp(scores - log_block).astype(jnp.bfloat16)
            head_block = jnp.einsum(
                "hqk,khd->qhd",
                attn_weights,
                split_heads(forward_value_rows),
                preferred_element_type=jnp.float32,
            )
            return (head_block.reshape(query_block.shape).astype(jnp.bfloat16), log_block)

        head_blocks, forward_log_total = lax.map(
            attend_block, (block_rows(forward_queries, block_len), block_rows(allowed, block_len))
        )
        head_out = head_blocks.reshape(forward_queries.shape)
        forward_attended = lax.all_to_all(head_out, "seq", split_axis=0, concat_axis=1, tiled=True)
        forward_residual = (
            layer_in
            + jnp.dot(forward_attended, forward_w_output, preferred_element_type=jnp.float32)
            + forward_bias_output.astype(jnp.float32)
        )
        forward_normed_two = layer_norm(
            forward_residual,
            forward_gain_two.astype(jnp.float32),
            forward_bias_two.astype(jnp.float32),
        ).astype(jnp.bfloat16)
        forward_pre_act = jnp.dot(
            forward_normed_two, forward_w_hidden, preferred_element_type=jnp.float32
        ) + forward_bias_hidden.astype(jnp.float32)
        forward_activated = gelu_tanh(forward_pre_act).astype(jnp.bfloat16)
        layer_out = (
            forward_residual
            + jnp.dot(forward_activated, forward_w_back, preferred_element_type=jnp.float32)
            + forward_bias_back.astype(jnp.float32)
        )
        forward_kept = (
            layer_in,
            forward_normed,
            forward_queries,
            forward_key_rows,
            forward_value_rows,
            forward_log_total,
            allowed,
            forward_attended,
            forward_residual,
            forward_normed_two,
            forward_pre_act,
            forward_activated,
        )
        layer_out, kept = (layer_out, forward_kept)
        kept_ticks.append(kept)
        layer_outs.append(layer_out)
        if tick_index < micro:
            received = shifted(layer_out.astype(jnp.bfloat16), "section", 1)
    sent_back = jnp.zeros((tok_rows, width), jnp.bfloat16)
    input_grads = []
    totals = None
    for tick_index in range(micro + 1):
        params = fetch_params()
        later = kept_ticks[min(tick_index + 1, micro)]
        earlier = kept_ticks[max(tick_index - 1, 0)]
        kept = jax.tree.map(
            lambda upper, lower: jnp.where(last_section, upper, lower), later, earlier
        )
        if tick_index < micro:
            top_grad = cotangent[tick_index].astype(jnp.float32)
        else:
            top_grad = jnp.zeros((tok_rows, width), jnp.float32)
        grad_out = jnp.where(last_section, top_grad, sent_back.astype(jnp.float32))
        (
            gain_one,
            bias_one,
            w_mixed,
            bias_query,
            bias_value,
            w_output,
            bias_output,
            gain_two,
            bias_two,
            w_hidden,
            bias_hidden,
            w_back,
            bias_back,
        ) = params
        (
            backward_layer_in,
            normed,
            queries,
            key_rows,
            value_rows,
            log_total,
            backward_allowed,
            attended,
            residual,
            normed_two,
            pre_act,
            activated,
        ) = kept
        grad_back = grad_out.astype(jnp.bfloat16)
        d_w_back = jnp.einsum("cf,cd->fd", activated, grad_back, preferred_element_type=jnp.float32)
        d_bias_back = jnp.sum(grad_back.astype(jnp.float32), axis=0)
        d_activated = jnp.einsum("cd,fd->cf", grad_back, w_back, preferred_element_type=jnp.float32)
        gelu_pull = jax.vjp(gelu_tanh, pre_act)[1]
        d_pre = gelu_pull(d_activated)[0].astype(jnp.bfloat16)
        d_w_hidden = jnp.einsum("cm,cf->mf", normed_two, d_pre, preferred_element_type=jnp.float32)
        d_bias_hidden = jnp.sum(d_pre.astype(jnp.float32), axis=0)
        d_normed_two = jnp.einsum("cf,mf->cm", d_pre, w_hidden, preferred_element_type=jnp.float32)
        norm_pull_two = jax.vjp(
            layer_norm, residual, gain_two.astype(jnp.float32), bias_two.astype(jnp.float32)
        )[1]
        d_resid_part, d_gain_two, d_bias_two = norm_pull_two(d_normed_two)
        d_residual = grad_out + d_resid_part
        grad_attn = d_residual.astype(jnp.bfloat16)
        d_w_output = jnp.einsum(
            "cm,cd->md", attended, grad_attn, preferred_element_type=jnp.float32
        )
        d_bias_output = jnp.sum(grad_attn.astype(jnp.float32), axis=0)
        d_attended = jnp.einsum(
            "cd,md->cm", grad_attn, w_output, preferred_element_type=jnp.float32
        ).astype(jnp.bfloat16)
        d_head = lax.all_to_all(d_attended, "seq", split_axis=1, concat_axis=0, tiled=True)

        def grad_block(carry, operands):
            key_acc, value_acc = carry
            query_block, head_grad_block, allowed_block, log_block = operands
            scores = masked_scores(query_block, key_rows, allowed_block)
            attn_probs = jnp.exp(scores - log_block)
            d_weights = jnp.einsum(
                "qhd,khd->hqk",
                split_heads(head_grad_block),
                split_heads(value_rows),
                preferred_element_type=jnp.float32,
            )
            row_dot = jnp.sum(attn_probs * d_weights, axis=-1, keepdims=True)
            d_scores = (attn_probs * (d_weights - row_dot) * score_scale).astype(jnp.bfloat16)
            d_query_block = (
                jnp.einsum(
                    "hqk,khd->qhd",
                    d_scores,
                    split_heads(key_rows),
                    preferred_element_type=jnp.float32,
                )
                .reshape(query_block.shape)
                .astype(jnp.bfloat16)
            )
            key_acc = key_acc + jnp.einsum(
                "hqk,qhd->khd",
                d_scores,
                split_heads(query_block),
                preferred_element_type=jnp.float32,
            ).reshape(key_rows.shape)
            value_acc = value_acc + jnp.einsum(
                "hqk,qhd->khd",
                attn_probs.astype(jnp.bfloat16),
                split_heads(head_grad_block),
                preferred_element_type=jnp.float32,
            ).reshape(value_rows.shape)
            return ((key_acc, value_acc), d_query_block)

        empty_terms = (
            jnp.zeros(key_rows.shape, jnp.float32),
            jnp.zeros(value_rows.shape, jnp.float32),
        )
        (key_term, value_term), query_blocks = lax.scan(
            grad_block,
            empty_terms,
            (
                block_rows(queries, block_len),
                block_rows(d_head, block_len),
                block_rows(backward_allowed, block_len),
                log_total,
            ),
        )
        d_query = query_blocks.reshape(queries.shape)
        d_key = lax.psum_scatter(key_term, "fsdp", scatter_dimension=0, tiled=True)
        d_value = lax.psum_scatter(value_term, "fsdp", scatter_dimension=0, tiled=True)
        d_heads = jnp.stack(
            [d_query, d_key.astype(jnp.bfloat16), d_value.astype(jnp.bfloat16)], axis=1
        )
        d_mixed = lax.all_to_all(d_heads, "seq", split_axis=0, concat_axis=2, tiled=True)
        d_flat = d_mixed.reshape(tok_rows, 3 * width)
        d_w_mixed = jnp.einsum("cm,cn->mn", normed, d_flat, preferred_element_type=jnp.float32)
        d_bias_query = jnp.sum(d_mixed[:, 0].astype(jnp.float32), axis=0)
        d_bias_value = jnp.sum(d_mixed[:, 2].astype(jnp.float32), axis=0)
        d_normed = jnp.einsum("cn,mn->cm", d_flat, w_mixed, preferred_element_type=jnp.float32)
        norm_pull_one = jax.vjp(
            layer_norm,
            backward_layer_in,
            gain_one.astype(jnp.float32),
            bias_one.astype(jnp.float32),
        )[1]
        d_in_part, d_gain_one, d_bias_one = norm_pull_one(d_normed)
        d_in = d_residual + d_in_part
        d_in, local_grads = (
            d_in,
            (
                d_gain_one,
                d_bias_one,
                d_w_mixed,
                d_bias_query,
                d_bias_value,
                d_w_output,
                d_bias_output,
                d_gain_two,
                d_bias_two,
                d_w_hidden,
                d_bias_hidden,
                d_w_back,
                d_bias_back,
            ),
        )
        input_grads.append(d_in)
        shared = (
            lax.psum_scatter(local_grads[0], ("seq", "fsdp"), scatter_dimension=0, tiled=True),
            lax.psum_scatter(local_grads[1], ("seq", "fsdp"), scatter_dimension=0, tiled=True),
            lax.psum_scatter(local_grads[2], ("seq", "fsdp"), scatter_dimension=0, tiled=True),
            lax.psum_scatter(local_grads[3], ("seq", "fsdp"), scatter_dimension=0, tiled=True),
            lax.psum_scatter(local_grads[4], ("seq", "fsdp"), scatter_dimension=0, tiled=True),
            lax.psum_scatter(local_grads[5], ("seq", "fsdp"), scatter_dimension=0, tiled=True),
            lax.psum_scatter(local_grads[6], ("seq", "fsdp"), scatter_dimension=0, tiled=True),
            lax.psum_scatter(local_grads[7], ("seq", "fsdp"), scatter_dimension=0, tiled=True),
            lax.psum_scatter(local_grads[8], ("seq", "fsdp"), scatter_dimension=0, tiled=True),
            lax.psum_scatter(local_grads[9], ("seq", "fsdp"), scatter_dimension=0, tiled=True),
            lax.psum_scatter(local_grads[10], ("seq", "fsdp"), scatter_dimension=0, tiled=True),
            lax.psum_scatter(local_grads[11], ("seq", "fsdp"), scatter_dimension=0, tiled=True),
            lax.psum_scatter(local_grads[12], ("seq", "fsdp"), scatter_dimension=0, tiled=True),
        )
        totals = shared if totals is None else jax.tree.map(jnp.add, totals, shared)
        if tick_index < micro:
            sent_back = shifted(d_in.astype(jnp.bfloat16), "section", -1)
    section_tops = jnp.stack(layer_outs[1:])
    bottom_grads = jnp.stack(input_grads[1:])
    relay_ends = jnp.where(last_section, section_tops, bottom_grads)[None]
    return (relay_ends,) + tuple((grad_part[None] for grad_part in totals))


def solution(mesh):
    placed = (
        P(None, ("seq", "fsdp"), None),
        P(None, ("seq", "fsdp"), None),
        P(),
        P("section", "fsdp"),
        P("section", "fsdp"),
        P("section", "fsdp", None),
        P("section", "fsdp"),
        P("section", "fsdp"),
        P("section", "fsdp", None),
        P("section", "fsdp"),
        P("section", "fsdp"),
        P("section", "fsdp"),
        P("section", "fsdp", None),
        P("section", "fsdp"),
        P("section", "fsdp", None),
        P("section", "fsdp"),
    )
    return jax.shard_map(
        body,
        mesh=mesh,
        in_specs=placed,
        out_specs=(
            P("section", None, ("seq", "fsdp"), None),
            P("section", ("seq", "fsdp")),
            P("section", ("seq", "fsdp")),
            P("section", ("seq", "fsdp"), None),
            P("section", ("seq", "fsdp")),
            P("section", ("seq", "fsdp")),
            P("section", ("seq", "fsdp"), None),
            P("section", ("seq", "fsdp")),
            P("section", ("seq", "fsdp")),
            P("section", ("seq", "fsdp")),
            P("section", ("seq", "fsdp"), None),
            P("section", ("seq", "fsdp")),
            P("section", ("seq", "fsdp"), None),
            P("section", ("seq", "fsdp")),
        ),
        check_vma=False,
    )
```

profile of v0, /device:TPU:0, one launch (start us, length us, event | category | flops | bytes accessed | tf_op | source)
XLA Modules:
  0.0 1992.8 jit_solution(17952211667077158032)
XLA Ops:
  10.1 12.6 all-gather.4
  30.5 11.9 all-gather.1
  42.4 8.4 all-gather
  52.3 75.6 %all-gather.24.cloned.1.call-done = bf16[1,1024,3072]{2,1,0:T(8,128)(2,1)} async-done(((bf16[1,256,3072]{2,1,0:T(8,128)(2,1)}), bf16[1,1024,3072]{2,1,0:T(8,128)(2,1)}) %all-gather.24.cloned.1.call-update) | async-done | bytes 6291472 | tf_op jit(solution)/shard_map/all_gather | solution.py:95
  146.6 21.7 %all-gather.5 = bf16[1024,1,256]{2,0,1:T(8,128)(2,1)S(1)} all-gather(bf16[256,1,256]{2,0,1:T(8,128)(2,1)S(1)} %get-tuple-element.260), channel_id=7, replica_groups=mesh['section'=2,'seq'=4,'fsdp'=4] {'fsdp'}, dimensions={0}, use_global_device_ids=true | all-gather | bytes 655360 | tf_op jit(solution)/shard_map/all_gather | solution.py:147
  168.6 21.3 %all-gather.6 = bf16[1024,1,256]{2,0,1:T(8,128)(2,1)S(1)} all-gather(bf16[256,1,256]{2,0,1:T(8,128)(2,1)S(1)} %get-tuple-element.258), channel_id=8, replica_groups=mesh['section'=2,'seq'=4,'fsdp'=4] {'fsdp'}, dimensions={0}, use_global_device_ids=true | all-gather | bytes 655360 | tf_op jit(solution)/shard_map/all_gather | solution.py:146
  197.9 8.7 all-gather.8
  206.7 10.6 all-gather.14
  217.3 13.3 all-gather.12
  230.6 10.7 all-gather.10
  241.3 10.1 all-gather.9
  253.9 86.8 %all-gather.28.cloned.1.call-done = bf16[1,1024,4096]{2,1,0:T(8,128)(2,1)} async-done(((bf16[1,256,4096]{2,1,0:T(8,128)(2,1)}), bf16[1,1024,4096]{2,1,0:T(8,128)(2,1)}) %all-gather.28.cloned.1.call-update) | async-done | bytes 8388624 | tf_op jit(solution)/shard_map/all_gather | solution.py:102
  345.8 144.3 %all-gather.30.cloned.1.call-done = bf16[1,4096,1024]{2,1,0:T(8,128)(2,1)} async-done(((bf16[1,1024,1024]{2,1,0:T(8,128)(2,1)}), bf16[1,4096,1024]{2,1,0:T(8,128)(2,1)}) %all-gather.30.cloned.1.call-update) | async-done | bytes 8388624 | tf_op jit(solution)/shard_map/all_gather | solution.py:104
  505.8 11.1 all_to_all.204
  518.2 15.8 all-gather.15
  535.0 15.9 all-gather.16
  561.0 8.7 all_to_all.205
  612.8 16.1 all-gather.17
  630.6 16.3 all-gather.18
  719.3 26.9 %reduce-scatter.11.cloned.1.call-done = f32[256,256]{1,0:T(8,128)} async-done(((f32[1024,256]{1,0:T(8,128)}), f32[256,256]{1,0:T(8,128)}) %reduce-scatter.11.cloned.1.call-update) | async-done | bytes 262160 | tf_op jit(solution)/shard_map/reduce_scatter | solution.py:328
  838.1 23.3 %reduce-scatter.15.cloned.1.call-done = f32[256,256]{1,0:T(8,128)} async-done(((f32[1024,256]{1,0:T(8,128)}), f32[256,256]{1,0:T(8,128)}) %reduce-scatter.15.cloned.1.call-update) | async-done | bytes 262160 | tf_op jit(solution)/shard_map/reduce_scatter | solution.py:328
  951.6 21.1 %reduce-scatter.19.cloned.1.call-done = f32[256,256]{1,0:T(8,128)} async-done(((f32[1024,256]{1,0:T(8,128)}), f32[256,256]{1,0:T(8,128)}) %reduce-scatter.19.cloned.1.call-update) | async-done | bytes 262160 | tf_op jit(solution)/shard_map/reduce_scatter | solution.py:328
  989.8 14.8 add_add_fusion.2
  1005.8 8.2 fusion.265
  1014.0 8.2 fusion.263
  1022.2 18.3 add_add_fusion.1
  1050.3 8.1 fusion.244
  1058.4 18.4 add_add_fusion
  1090.1 78.2 %all-reduce.9 = (f32[1024]{0:T(1024)S(1)}, f32[1024]{0:T(1024)S(1)}, f32[1024]{0:T(1024)S(1)}, f32[1024]{0:T(1024)S(1)}, f32[1024]{0:T(1024)S(1)}, /*index=5*/f3...) all-reduce(f32[1024]{0:T(1024)S(1)} %add_add_fusion.21, ...), channel_id=53, replica_groups=mesh['section'=2,'seq'=4,'fsdp'=4] {'seq','fsdp'}, use_global_device_ids=true, to_apply=%region_52.53.clone | all-reduce | flops 12288 | bytes 98304
  1174.5 107.1 %reduce-scatter.23.cloned.1.call-done = f32[64,3072]{1,0:T(8,128)} async-done(((f32[1024,3072]{1,0:T(8,128)}), f32[64,3072]{1,0:T(8,128)}) %reduce-scatter.23.cloned.1.call-update) | async-done | bytes 786448 | tf_op jit(solution)/shard_map/reduce_scatter | solution.py:369
  1281.6 352.7 %reduce-scatter.27.cloned.1.call-done = f32[64,4096]{1,0:T(8,128)} async-done(((f32[1024,4096]{1,0:T(8,128)}), f32[64,4096]{1,0:T(8,128)}) %reduce-scatter.27.cloned.1.call-update) | async-done | bytes 1048592 | tf_op jit(solution)/shard_map/reduce_scatter | solution.py:376
  1634.2 351.9 %reduce-scatter.29.cloned.1.call-done = f32[256,1024]{1,0:T(8,128)} async-done(((f32[4096,1024]{1,0:T(8,128)}), f32[256,1024]{1,0:T(8,128)}) %reduce-scatter.29.cloned.1.call-update) | async-done | bytes 1048592 | tf_op jit(solution)/shard_map/reduce_scatter | solution.py:378
  (696 shorter events, 418.1 us)
Async XLA Ops:
  7.2 120.6 %all-gather.24.cloned.1.call-start = ((), (), s32[]{:S(2)}) async-start(), calls=%async_computation.28 | async-start | bytes 7864320 | tf_op jit(solution)/shard_map/all_gather | solution.py:95
  8.0 243.5 %all-gather.26.cloned.1.call-start = ((), (), s32[]{:S(2)}) async-start(), calls=%async_computation.29 | async-start | bytes 2621440 | tf_op jit(solution)/shard_map/all_gather | solution.py:98
  8.7 332.0 %all-gather.28.cloned.1.call-start = ((), (), s32[]{:S(2)}) async-start(), calls=%async_computation.30 | async-start | bytes 10485760 | tf_op jit(solution)/shard_map/all_gather | solution.py:102
  9.5 480.7 %all-gather.30.cloned.1.call-start = ((), (), s32[]{:S(2)}) async-start(), calls=%async_computation.31 | async-start | bytes 10485760 | tf_op jit(solution)/shard_map/all_gather | solution.py:104
  134.8 10.5 all-to-all-start
  140.5 411.6 %copy-start.50 = (pred[256,1024]{1,0:T(8,128)(4,1)}, pred[256,1024]{1,0:T(8,128)(4,1)S(1)}, u32[]{:S(2)}) copy-start(pred[256,1024]{1,0:T(8,128)(4,1)S(1)} %get-tuple-element.270) | copy-start | bytes 786436
  194.6 56.8 %all-to-all-start.1 = ((bf16[4,64,256]{2,1,0:T(8,128)(2,1)}), bf16[4,64,256]{2,1,0:T(8,128)(2,1)S(1)}, u32[]{:S(2)}, u32[]{:S(2)}) async-start(bf16[4,64,256]{2,1,0:T(8,128)(2,1)} %copy.335), calls=%async_computation.1 | async-start | bytes 262144 | tf_op jit(solution)/shard_map/all_to_all | solution.py:169
  217.3 272.9 %copy-start.95 = (f32[1,1024]{1,0:T(1,128)}, f32[1,1024]{1,0:T(1,128)S(1)}, u32[]{:S(2)}) copy-start(f32[1,1024]{1,0:T(1,128)S(1)} %convert_element_type.460) | copy-start | bytes 12292
  253.7 236.4 %copy-start.8 = (f32[64,1024]{1,0:T(8,128)}, f32[64,1024]{1,0:T(8,128)S(1)}, u32[]{:S(2)}) copy-start(f32[64,1024]{1,0:T(8,128)S(1)} %get-tuple-element.277) | copy-start | bytes 786436
  345.8 254.7 %copy-start.1 = (f32[64,4096]{1,0:T(8,128)}, f32[64,4096]{1,0:T(8,128)S(1)}, u32[]{:S(2)}) copy-start(f32[64,4096]{1,0:T(8,128)S(1)} %fusion.39) | copy-start | bytes 3145732
  495.1 2.9 collective-permute-start
  582.7 2.3 collective-permute-start.1
  596.3 11.9 all-to-all-start.4
  654.7 9.5 all-to-all-start.5
  678.2 9.1 all-to-all-start.6
  682.3 36.0 %reduce-scatter.13.cloned.1.call-start = ((), (), s32[]{:S(2)}) async-start(), calls=%async_computation.23 | async-start | bytes 1310720 | tf_op jit(solution)/shard_map/reduce_scatter | solution.py:329
  692.4 53.8 %reduce-scatter.11.cloned.1.call-start = ((), (), s32[]{:S(2)}) async-start(), calls=%async_computation.22 | async-start | bytes 1310720 | tf_op jit(solution)/shard_map/reduce_scatter | solution.py:328
  748.3 12.4 all-to-all-start.7
  771.8 3.2 collective-permute-start.2
  788.4 9.2 all-to-all-start.8
  792.3 44.2 %reduce-scatter.17.cloned.1.call-start = ((), (), s32[]{:S(2)}) async-start(), calls=%async_computation.25 | async-start | bytes 1310720 | tf_op jit(solution)/shard_map/reduce_scatter | solution.py:329
  807.4 54.0 %reduce-scatter.15.cloned.1.call-start = ((), (), s32[]{:S(2)}) async-start(), calls=%async_computation.24 | async-start | bytes 1310720 | tf_op jit(solution)/shard_map/reduce_scatter | solution.py:328
  864.5 12.5 all-to-all-start.9
  890.0 3.2 collective-permute-start.3
  905.8 8.6 all-to-all-start.10
  909.2 41.4 %reduce-scatter.21.cloned.1.call-start = ((), (), s32[]{:S(2)}) async-start(), calls=%async_computation.27 | async-start | bytes 1310720 | tf_op jit(solution)/shard_map/reduce_scatter | solution.py:329
  918.9 53.9 %reduce-scatter.19.cloned.1.call-start = ((), (), s32[]{:S(2)}) async-start(), calls=%async_computation.26 | async-start | bytes 1310720 | tf_op jit(solution)/shard_map/reduce_scatter | solution.py:328
  931.5 243.0 %reduce-scatter.25.cloned.1.call-start = ((), (), s32[]{:S(2)}) async-start(), calls=%async_computation.33 | async-start | bytes 4456448 | tf_op jit(solution)/shard_map/reduce_scatter | solution.py:372
  974.9 13.4 all-to-all-start.11
  978.6 303.0 %reduce-scatter.23.cloned.1.call-start = ((), (), s32[]{:S(2)}) async-start(), calls=%async_computation.32 | async-start | bytes 13369344 | tf_op jit(solution)/shard_map/reduce_scatter | solution.py:369
  1004.7 629.5 %reduce-scatter.27.cloned.1.call-start = ((), (), s32[]{:S(2)}) async-start(), calls=%async_computation.34 | async-start | bytes 17825792 | tf_op jit(solution)/shard_map/reduce_scatter | solution.py:376
  1040.6 945.5 %reduce-scatter.29.cloned.1.call-start = ((), (), s32[]{:S(2)}) async-start(), calls=%async_computation.35 | async-start | bytes 17825792 | tf_op jit(solution)/shard_map/reduce_scatter | solution.py:378
  (179 other events, 2454.9 us)
Sparse Core Ops, SparseCore 0:
  9.6 118.1 all-gather.23
  129.4 60.7 all-gather.25
  191.8 148.8 all-gather.27
  342.1 147.9 all-gather.29
  692.5 25.5 reduce-scatter.12
  720.3 25.7 reduce-scatter.10
  807.5 25.6 reduce-scatter.16
  835.5 25.7 reduce-scatter.14
  919.0 25.6 reduce-scatter.20
  946.9 25.7 reduce-scatter.18
  975.6 95.0 reduce-scatter.24
  1076.8 204.7 reduce-scatter.22
  1284.5 349.6 reduce-scatter.26
  1637.1 348.9 reduce-scatter.28
where the time goes:
time: 2000 us; the launch traced here: 1990 us
  waiting for transfers between devices  1220 us (61%)
  blocking collectives  299 us (15%)
  matrix products  287 us (14%)
  local copies, waits for them, and re-layouts  88.8 us (4%)
  starting transfers between devices  46.1 us (2%)
  other arithmetic  37.7 us (2%)
    reduce_scatter x1, waiting for transfers between devices, body(): lax.psum_scatter(local_grads[9], ('seq', 'fsdp'), scatter_dimension=0, ti...  353 us
    reduce_scatter x1, waiting for transfers between devices, body(): lax.psum_scatter(local_grads[11], ('seq', 'fsdp'), scatter_dimension=0, t...  352 us
    all_gather x1, waiting for transfers between devices, fetch_params(): lax.all_gather(w_proj[0], 'fsdp', axis=0, tiled=True)  144 us
    reduce_scatter x1, waiting for transfers between devices, body(): lax.psum_scatter(local_grads[2], ('seq', 'fsdp'), scatter_dimension=0, ti...  107 us
    all_gather x1, waiting for transfers between devices, fetch_params(): lax.all_gather(w_fc[0], 'fsdp', axis=0, tiled=True)  86.8 us
    unnamed x1, blocking collectives  78.2 us
    all_gather x1, waiting for transfers between devices, fetch_params(): lax.all_gather(w_qkv[0], 'fsdp', axis=0, tiled=True)  75.6 us
    reduce_scatter x3, waiting for transfers between devices, body(): d_key = lax.psum_scatter(key_term, 'fsdp', scatter_dimension=0, tiled=True)  71.3 us
  transfers between devices with their start and end apart: 28, of which 20 were waited for; matrix products, arithmetic and copies ran while one was open for 13% of the time, Pallas kernels for 0%

commit v1 on v0

--- a/solution.py
+++ b/solution.py
@@ -3,6 +3,8 @@
 import jax
 import jax.numpy as jnp
 from jax import lax
+from jax.experimental import pallas as pl
+from jax.experimental.pallas import tpu as pltpu
 from jax.sharding import PartitionSpec as P
 
 DH = 64
@@ -387,6 +389,894 @@
     return (relay_ends,) + tuple((grad_part[None] for grad_part in totals))
 
 
+BF = jnp.bfloat16
+F32 = jnp.float32
+GROUP = 4
+KERNEL_VMEM = 56 * 1024 * 1024
+
+
+def nt(left, right):
+    return lax.dot_general(left, right, (((1,), (1,)), ((), ())), preferred_element_type=F32)
+
+
+def tn(left, right):
+    return lax.dot_general(left, right, (((0,), (0,)), ((), ())), preferred_element_type=F32)
+
+
+def nn(left, right):
+    return jnp.dot(left, right, preferred_element_type=F32)
+
+
+def spot(start, size):
+    return pl.ds(pl.multiple_of(start, size), size)
+
+
+def call(kernel, name, ids, args, outs, scratch=(), anywhere=(), cost=None):
+    where = [pl.ANY if i in anywhere else pltpu.VMEM for i in range(len(args))]
+    flops, nbytes = cost or (0, 0)
+    nbytes = nbytes or sum(a.size * a.dtype.itemsize for a in args)
+    return pl.pallas_call(
+        kernel,
+        name=name,
+        out_shape=[jax.ShapeDtypeStruct(shape, dtype) for shape, dtype in outs],
+        in_specs=[pl.BlockSpec(memory_space=pltpu.SMEM)]
+        + [pl.BlockSpec(memory_space=space) for space in where],
+        out_specs=[pl.BlockSpec(memory_space=pltpu.VMEM)] * len(outs),
+        scratch_shapes=list(scratch),
+        compiler_params=pltpu.CompilerParams(vmem_limit_bytes=KERNEL_VMEM),
+        cost_estimate=pl.CostEstimate(flops=flops, bytes_accessed=nbytes, transcendentals=0),
+    )(ids, *args)
+
+
+def trade(blocks, axis):
+    got = [blocks[0]]
+    for d in range(1, GROUP):
+        got.append(lax.ppermute(blocks[d], axis, [(i, i ^ d) for i in range(GROUP)]))
+    return got
+
+
+def gather(block, axis):
+    return trade([block] * GROUP, axis)
+
+
+def swap(block):
+    return lax.ppermute(block, "section", [(0, 1), (1, 0)])
+
+
+def normed_rows(values, gain_vec, bias_vec):
+    average = jnp.mean(values, axis=-1, keepdims=True)
+    centred = values - average
+    variance = jnp.mean(centred * centred, axis=-1, keepdims=True)
+    return centred * lax.rsqrt(variance + EPSILON) * gain_vec + bias_vec
+
+
+def norm_pull(values, gain_vec, grad):
+    average = jnp.mean(values, axis=-1, keepdims=True)
+    centred = values - average
+    variance = jnp.mean(centred * centred, axis=-1, keepdims=True)
+    inverse = lax.rsqrt(variance + EPSILON)
+    unit = centred * inverse
+    scaled = grad * gain_vec
+    first = jnp.mean(scaled, axis=-1, keepdims=True)
+    second = jnp.mean(scaled * unit, axis=-1, keepdims=True)
+    pulled = inverse * (scaled - first - unit * second)
+    return (
+        pulled,
+        jnp.sum(grad * unit, axis=0, keepdims=True),
+        jnp.sum(grad, axis=0, keepdims=True),
+    )
+
+
+def pick_mixed_kernel(ids, w_ref, mine_ref, send_ref, tiles, sem):
+    s, c = ids[0], ids[2]
+    width = w_ref.shape[2] // 3
+    odd = (s & 1) == 1
+    copies = []
+    for t in range(3):
+        for j in range(GROUP):
+            start = t * width + j * 256 + (s >> 1) * 128
+            copy = pltpu.make_async_copy(
+                w_ref.at[0, :, spot(start, 128)], tiles.at[t, j], sem.at[t * GROUP + j]
+            )
+            copy.start()
+            copies.append(copy)
+    for copy in copies:
+        copy.wait()
+
+    def head(t, j):
+        tile = tiles[t, j].astype(F32)
+        return jnp.where(odd, tile[:, DH:], tile[:, :DH])
+
+    def fill(ref, half):
+        for i in range(2):
+            j = 2 * half + i
+            ref[:, i * 128 : i * 128 + 128] = jnp.concatenate(
+                [head(0, j), head(1, j)], axis=1
+            ).astype(BF)
+        ref[:, 256:384] = jnp.concatenate(
+            [head(2, 2 * half), head(2, 2 * half + 1)], axis=1
+        ).astype(BF)
+
+    fill(mine_ref, c)
+    fill(send_ref, 1 - c)
+
+
+def pick_rest_kernel(ids, fc_ref, proj_ref, out_ref, a_mine, a_send, p_mine, p_send, sem):
+    s, c = ids[0], ids[2]
+    copies = []
+
+    def begin(source, target):
+        copy = pltpu.make_async_copy(source, target, sem.at[len(copies)])
+        copy.start()
+        copies.append(copy)
+
+    for a_ref, p_ref, half in ((a_mine, p_mine, c), (a_send, p_send, 1 - c)):
+        begin(out_ref.at[0, spot(s * 64, 64), spot(half * 512, 512)], a_ref.at[0:64, :])
+        for j in range(GROUP):
+            start = j * 1024 + s * 256 + half * 128
+            begin(
+                fc_ref.at[0, :, spot(start, 128)],
+                a_ref.at[64:320, j * 128 : (j + 1) * 128],
+            )
+        begin(proj_ref.at[0, spot(s * 256 + half * 128, 128), :], p_ref)
+    for copy in copies:
+        copy.wait()
+
+
+def mixed_kernel(ids, *refs):
+    x_refs, own_refs, oth_refs = refs[:4], refs[4:8], refs[8:12]
+    vec = refs[12]
+    out_refs, nf_ref = refs[13:17], refs[17]
+    packed = refs[18]
+    s, z, c = ids[0], ids[1], ids[2]
+    gain_vec, bias_vec = vec[0:1, :], vec[1:2, :]
+    for d in range(GROUP):
+        nf_ref[d * 64 : (d + 1) * 64, :] = normed_rows(
+            x_refs[d][...].astype(F32), gain_vec, bias_vec
+        ).astype(BF)
+
+    def bias_of(row, j):
+        tile = vec[row : row + 1, spot(j * 256 + (s >> 1) * 128, 128)]
+        return jnp.where((s & 1) == 1, tile[:, DH:], tile[:, :DH])
+
+    empty = jnp.zeros((1, DH), F32)
+    for w_refs, half in ((own_refs, c), (oth_refs, 1 - c)):
+        total = jnp.zeros((GROUP * 64, 384), F32)
+        for d in range(GROUP):
+            total = total + nn(nf_ref[:, spot((z ^ d) * 256, 256)], w_refs[d][...])
+        j = 2 * half
+        row = jnp.concatenate(
+            [
+                bias_of(2, j),
+                empty,
+                bias_of(2, j + 1),
+                empty,
+                bias_of(3, j),
+                bias_of(3, j + 1),
+            ],
+            axis=1,
+        )
+        total = total + row
+        for i in range(2):
+            packed[j + i, 0:256, :] = total[:, i * 128 : (i + 1) * 128].astype(BF)
+            values = total[:, 256 + i * DH : 256 + (i + 1) * DH]
+            packed[j + i, 256:384, :] = jnp.concatenate(
+                [values[:128], values[128:]], axis=1
+            ).astype(BF)
+    for d in range(GROUP):
+        out_refs[d][...] = packed[z ^ d]
+
+
+def spread(ids, pieces, qk_ref, v_ref):
+    s, z = ids[0], ids[1]
+    for d in range(GROUP):
+        for e in range(GROUP):
+            rows = spot(((s ^ e) * GROUP + (z ^ d)) * 64, 64)
+            qk_ref[rows, :] = pieces[d][e * 64 : (e + 1) * 64, :]
+            lanes = slice(0, DH) if e < 2 else slice(DH, 128)
+            start = 256 + (e & 1) * 64
+            v_ref[rows, :] = pieces[d][start : start + 64, lanes]
+
+
+def block_scores(qk_ref, seg_col, seg_row, start, size):
+    stop = start + size
+    queries = qk_ref[start:stop, 0:DH] * jnp.asarray(DH ** (-0.5), BF)
+    scores = nt(queries, qk_ref[0:stop, DH:128])
+    q_place = lax.broadcasted_iota(jnp.int32, (size, stop), 0) + start
+    k_place = lax.broadcasted_iota(jnp.int32, (size, stop), 1)
+    q_doc, k_doc = seg_col[start:stop, :], seg_row[:, 0:stop]
+    same = (q_doc == k_doc) & (q_doc > 0)
+    allowed = ((k_place <= q_place) & same) | (k_place == q_place)
+    return jnp.where(allowed, scores, NEGATIVE)
+
+
+def attend_kernel(ids, *refs):
+    pieces, seg_col, seg_row = refs[:4], refs[4], refs[5]
+    out_refs = refs[6:10]
+    qk_ref, v_ref, o_ref = refs[10:13]
+    s, z = ids[0], ids[1]
+    spread(ids, pieces, qk_ref, v_ref)
+    count = qk_ref.shape[0]
+    size = 256
+    for start in range(0, count, size):
+        scores = block_scores(qk_ref, seg_col, seg_row, start, size)
+        top = jnp.max(scores, axis=-1, keepdims=True)
+        grown = jnp.exp(scores - top)
+        total = jnp.sum(grown, axis=-1, keepdims=True)
+        mixed = nn(grown.astype(BF), v_ref[0 : start + size, :])
+        o_ref[start : start + size, :] = (mixed / total).astype(BF)
+    for d in range(GROUP):
+        for e in range(2):
+            left = o_ref[spot(((s ^ e) * GROUP + (z ^ d)) * 64, 64), :]
+            right = o_ref[spot(((s ^ (e + 2)) * GROUP + (z ^ d)) * 64, 64), :]
+            out_refs[d][e * 64 : (e + 1) * 64, :] = jnp.concatenate([left, right], axis=1)
+
+
+def unpacked(piece):
+    return jnp.concatenate([piece[:, :DH], piece[:, DH:]], axis=0)
+
+
+def head_rows(w_ref, z):
+    return jnp.concatenate([w_ref[z ^ d, 0:64, :] for d in range(GROUP)], axis=0)
+
+
+def output_kernel(ids, *refs):
+    pieces, own_ref, oth_ref = refs[:4], refs[4], refs[5]
+    out_refs, att_ref = refs[6:10], refs[10]
+    z, c = ids[1], ids[2]
+    att = jnp.concatenate([unpacked(pieces[d][...]) for d in range(GROUP)], axis=1)
+    att_ref[...] = att
+    for w_ref, half in ((own_ref, c), (oth_ref, 1 - c)):
+        part = nn(att, head_rows(w_ref, z)).astype(BF)
+        for d in range(GROUP):
+            out_refs[d][:, spot(half * 512, 512)] = part[d * 64 : (d + 1) * 64, :]
+
+
+def summed(refs):
+    total = refs[0][...].astype(F32)
+    for ref in refs[1:]:
+        total = total + ref[...].astype(F32)
+    return total
+
+
+def residual_kernel(ids, *refs):
+    x_ref, vec = refs[4], refs[5]
+    res_ref, n_ref = refs[6], refs[7]
+    res = x_ref[...].astype(F32) + summed(refs[:4]) + vec[4:5, :]
+    res_ref[...] = res
+    n_ref[...] = normed_rows(res, vec[5:6, :], vec[6:7, :]).astype(BF)
+
+
+ROOT = math.sqrt(2.0 / math.pi)
+
+
+def hidden_bias(vec, half):
+    return jnp.concatenate(
+        [vec[8:9, spot(j * 256 + half * 128, 128)] for j in range(GROUP)], axis=1
+    )
+
+
+def feed_kernel(ids, *refs):
+    n_refs, a_refs, p_refs, vec = refs[:4], refs[4:6], refs[6:8], refs[8]
+    out_refs = refs[9:13]
+    slope_ref, act_ref, nf_ref = refs[13:16]
+    c = ids[2]
+    for d in range(GROUP):
+        nf_ref[d * 64 : (d + 1) * 64, :] = n_refs[d][...]
+    part = jnp.zeros(nf_ref.shape, F32)
+    for place, half in ((0, c), (1, 1 - c)):
+        cols = slice(place * 512, (place + 1) * 512)
+        pre = jnp.zeros((GROUP * 64, 512), F32)
+        for k in range(GROUP):
+            pre = pre + nn(nf_ref[:, k * 256 : (k + 1) * 256], a_refs[place][k, 64:320, :])
+        pre = pre + hidden_bias(vec, half)
+        square = pre * pre
+        bend = jnp.tanh(ROOT * pre * (1.0 + 0.044715 * square))
+        act = (0.5 * pre * (1.0 + bend)).astype(BF)
+        slope_ref[:, cols] = 0.5 * (1.0 + bend) + (0.5 * ROOT) * pre * (1.0 - bend * bend) * (
+            1.0 + (3.0 * 0.044715) * square
+        )
+        act_ref[:, cols] = act
+        w_back = p_refs[place][...].reshape(512, nf_ref.shape[1])
+        part = part + nn(act, w_back)
+    for d in range(GROUP):
+        out_refs[d][...] = part[d * 64 : (d + 1) * 64, :].astype(BF)
+
+
+def close_kernel(ids, *refs):
+    res_ref, vec = refs[4], refs[5]
+    out_ref, low_ref = refs[6], refs[7]
+    out = res_ref[...] + summed(refs[:4]) + vec[7:8, :]
+    out_ref[...] = out
+    low_ref[...] = out.astype(BF)
+
+
+def feed_back_kernel(ids, *refs):
+    g_refs, a_refs, p_refs, slope_ref = refs[:4], refs[4:6], refs[6:8], refs[8]
+    out_refs = refs[9:13]
+    d_pre_ref, gf_ref = refs[13:15]
+    for d in range(GROUP):
+        gf_ref[d * 64 : (d + 1) * 64, :] = g_refs[d][...]
+    for place in range(2):
+        cols = slice(place * 512, (place + 1) * 512)
+        w_back = p_refs[place][...].reshape(512, gf_ref.shape[1])
+        d_pre_ref[:, cols] = (nt(gf_ref[...], w_back) * slope_ref[:, cols]).astype(BF)
+    for k in range(GROUP):
+        part = nt(d_pre_ref[:, 0:512], a_refs[0][k, 64:320, :])
+        part = (part + nt(d_pre_ref[:, 512:1024], a_refs[1][k, 64:320, :])).astype(BF)
+        for d in range(GROUP):
+            out_refs[d][:, k * 256 : (k + 1) * 256] = part[d * 64 : (d + 1) * 64, :]
+
+
+def norm_two_back_kernel(ids, *refs):
+    res_ref, g_ref, vec = refs[4], refs[5], refs[6]
+    d_res_ref, ga_ref, rows_ref = refs[7:10]
+    grad = g_ref[...].astype(F32)
+    pulled, d_gain, d_bias = norm_pull(res_ref[...], vec[5:6, :], summed(refs[:4]))
+    d_res = grad + pulled
+    low = d_res.astype(BF)
+    d_res_ref[...] = d_res
+    ga_ref[...] = low
+    rows_ref[0:1, :] = jnp.sum(low.astype(F32), axis=0, keepdims=True)
+    rows_ref[1:2, :] = d_gain
+    rows_ref[2:3, :] = d_bias
+    rows_ref[3:4, :] = jnp.sum(grad.astype(BF).astype(F32), axis=0, keepdims=True)
+    rows_ref[4:8, :] = jnp.zeros((4, grad.shape[1]), F32)
+
+
+def output_back_kernel(ids, *refs):
+    g_refs, own_ref, oth_ref = refs[:4], refs[4], refs[5]
+    out_refs, gf_ref = refs[6:10], refs[10]
+    z, c = ids[1], ids[2]
+    for d in range(GROUP):
+        gf_ref[d * 64 : (d + 1) * 64, :] = g_refs[d][...]
+    d_att = nt(gf_ref[:, spot(c * 512, 512)], head_rows(own_ref, z))
+    d_att = d_att + nt(gf_ref[:, spot((1 - c) * 512, 512)], head_rows(oth_ref, z))
+    for d in range(GROUP):
+        cols = d_att[:, d * DH : (d + 1) * DH]
+        out_refs[d][...] = jnp.concatenate([cols[:128], cols[128:]], axis=1).astype(BF)
+
+
+def feed_grads_kernel(ids, *refs):
+    act_ref, gb_ref, nf_ref, d_pre_ref, att_ref, ga_ref = refs[:6]
+    keep_ref, send_ref, sums_ref = refs[6:9]
+    z, c = ids[1], ids[2]
+    width = gb_ref.shape[1]
+    for place, out_ref, half in ((0, keep_ref, c), (1, send_ref, 1 - c)):
+        cols = slice(place * 512, (place + 1) * 512)
+        d_fc = tn(nf_ref[...], d_pre_ref[:, cols]).astype(BF)
+        for o in range(width // 64):
+            out_ref[o % GROUP, (o // GROUP) * 64 : (o // GROUP) * 64 + 64, :] = d_fc[
+                o * 64 : (o + 1) * 64, :
+            ]
+        d_proj = tn(act_ref[:, cols], gb_ref[...]).astype(BF)
+        for j in range(GROUP):
+            rows = d_proj[j * 128 : (j + 1) * 128, :]
+            out_ref[j, 256:384, :] = rows[:, 0:512]
+            out_ref[j, 384:512, :] = rows[:, 512:1024]
+        d_out = tn(att_ref[...], ga_ref[:, spot(half * 512, 512)]).astype(BF)
+        for d in range(GROUP):
+            out_ref[z ^ d, 512:576, :] = d_out[d * 64 : (d + 1) * 64, :]
+    sums_ref[...] = jnp.sum(d_pre_ref[...].astype(F32), axis=0, keepdims=True)
+
+
+def attend_back_kernel(ids, *refs):
+    pieces, d_pieces, seg_col, seg_row = refs[:4], refs[4:8], refs[8], refs[9]
+    out_refs = refs[10:14]
+    qk_ref, v_ref, do_ref, dq_ref, dk_ref, dv_ref = refs[14:20]
+    s, z = ids[0], ids[1]
+    spread(ids, pieces, qk_ref, v_ref)
+    for d in range(GROUP):
+        for e in range(GROUP):
+            rows = spot(((s ^ e) * GROUP + (z ^ d)) * 64, 64)
+            lanes = slice(0, DH) if e < 2 else slice(DH, 128)
+            start = (e & 1) * 64
+            do_ref[rows, :] = d_pieces[d][start : start + 64, lanes]
+    count = qk_ref.shape[0]
+    size = 256
+    for start in range(0, count, size):
+        stop = start + size
+        scores = block_scores(qk_ref, seg_col, seg_row, start, size)
+        top = jnp.max(scores, axis=-1, keepdims=True)
+        grown = jnp.exp(scores - top)
+        probs = grown * (1.0 / jnp.sum(grown, axis=-1, keepdims=True))
+        d_out = do_ref[start:stop, :]
+        d_weights = nt(d_out, v_ref[0:stop, :])
+        row_dot = jnp.sum(probs * d_weights, axis=-1, keepdims=True)
+        d_scores = (probs * (d_weights - row_dot) * DH ** (-0.5)).astype(BF)
+        dq_ref[start:stop, :] = nn(d_scores, qk_ref[0:stop, DH:128])
+        dk = tn(d_scores, qk_ref[start:stop, 0:DH])
+        dv = tn(probs.astype(BF), d_out)
+        if start:
+            dk_ref[0:start, :] += dk[0:start]
+            dv_ref[0:start, :] += dv[0:start]
+        dk_ref[start:stop, :] = dk[start:stop]
+        dv_ref[start:stop, :] = dv[start:stop]
+    for d in range(GROUP):
+        for e in range(GROUP):
+            rows = spot(((s ^ e) * GROUP + (z ^ d)) * 64, 64)
+            out_refs[d][e * 64 : (e + 1) * 64, :] = jnp.concatenate(
+                [dq_ref[rows, :], dk_ref[rows, :]], axis=1
+            ).astype(BF)
+        for e in range(2):
+            left = dv_ref[spot(((s ^ e) * GROUP + (z ^ d)) * 64, 64), :]
+            right = dv_ref[spot(((s ^ (e + 2)) * GROUP + (z ^ d)) * 64, 64), :]
+            out_refs[d][256 + e * 64 : 320 + e * 64, :] = jnp.concatenate(
+                [left, right], axis=1
+            ).astype(BF)
+
+
+def mixed_back_kernel(ids, *refs):
+    pieces, own_refs, oth_refs = refs[:4], refs[4:8], refs[8:12]
+    out_refs, dm_ref = refs[12:16], refs[16]
+    held = refs[17]
+    z, c = ids[1], ids[2]
+    for d in range(GROUP):
+        held[d] = pieces[d][...]
+    for place, half in ((0, c), (1, 1 - c)):
+        base = place * 384
+        values = []
+        for i in range(2):
+            d = (2 * half + i) ^ z
+            dm_ref[:, base + i * 128 : base + (i + 1) * 128] = held[d, 0:256, :]
+            values.append(unpacked(held[d, 256:384, :]))
+        dm_ref[:, base + 256 : base + 384] = jnp.concatenate(values, axis=1)
+    for k in range(GROUP):
+        part = nt(dm_ref[:, 0:384], own_refs[k][...])
+        part = (part + nt(dm_ref[:, 384:768], oth_refs[k][...])).astype(BF)
+        for d in range(GROUP):
+            out_refs[d][:, spot((z ^ k) * 256, 256)] = part[d * 64 : (d + 1) * 64, :]
+
+
+def mixed_grads_kernel(ids, *refs):
+    nf_ref, dm_ref = refs[:2]
+    keep_refs, send_refs, sums_ref = refs[2:6], refs[6:10], refs[10]
+    held = refs[11]
+    z = ids[1]
+    for out_refs, cols in ((keep_refs, slice(0, 384)), (send_refs, slice(384, 768))):
+        d_w = tn(nf_ref[...], dm_ref[:, cols]).astype(BF)
+        for o in range(nf_ref.shape[1] // 64):
+            held[o % GROUP, (o // GROUP) * 64 : (o // GROUP) * 64 + 64, :] = d_w[
+                o * 64 : (o + 1) * 64, :
+            ]
+        for d in range(GROUP):
+            out_refs[d][...] = held[z ^ d]
+    sums_ref[...] = jnp.sum(dm_ref[...].astype(F32), axis=0, keepdims=True)
+
+
+def norm_one_back_kernel(ids, *refs):
+    x_ref, d_res_ref, vec = refs[4], refs[5], refs[6]
+    d_in_ref, low_ref, rows_ref = refs[7:10]
+    pulled, d_gain, d_bias = norm_pull(x_ref[...].astype(F32), vec[0:1, :], summed(refs[:4]))
+    d_in = d_res_ref[...] + pulled
+    d_in_ref[...] = d_in
+    low_ref[...] = d_in.astype(BF)
+    rows_ref[0:1, :] = d_gain
+    rows_ref[1:2, :] = d_bias
+    rows_ref[2:8, :] = jnp.zeros((6, d_in.shape[1]), F32)
+
+
+def add_kernel(ids, *refs):
+    count = len(refs) // 3
+    for k in range(count):
+        left, right = refs[k][...], refs[count + k][...]
+        refs[2 * count + k][...] = (left.astype(F32) + right.astype(F32)).astype(BF)
+
+
+def split_mixed_kernel(ids, *refs):
+    out_refs, held = refs[4:8], refs[8]
+    held[...] = summed(refs[:4]).astype(BF)
+    for d in range(GROUP):
+        out_refs[d][...] = held[spot((ids[0] ^ d) * 64, 64), :]
+
+
+def split_feed_kernel(ids, got_ref, o0, o1, o2, o3, po_ref):
+    for d, ref in enumerate((o0, o1, o2, o3)):
+        ref[...] = got_ref[spot((ids[0] ^ d) * 64, 64), :]
+    po_ref[...] = got_ref[256:576, :]
+
+
+def pack_kernel(ids, *refs):
+    fc, mixed, out_ref = refs[:4], refs[4:8], refs[8]
+    for d in range(GROUP):
+        source = ids[0] ^ d
+        out_ref[:, spot(source * 512, 512)] = fc[d][...]
+        start = pl.multiple_of(2048 + source * 384, 128)
+        out_ref[:, pl.ds(start, 384)] = mixed[d][...]
+
+
+def rows_kernel(ids, *refs):
+    layers, keep_ref, send_ref = (refs[:4], refs[4:8]), refs[8], refs[9]
+    held = refs[10]
+    s, c = ids[0], ids[2]
+    for index, (two_ref, one_ref, fc_ref, mixed_ref) in enumerate(layers):
+        held[index] = jnp.zeros(held.shape[1:], F32)
+        held[index, 0:2, :] = one_ref[0:2, :]
+        held[index, 2:6, :] = two_ref[0:4, :]
+        for place, half in ((0, c), (1, 1 - c)):
+            for j in range(GROUP):
+                start = place * 512 + j * 128
+                held[index, 8 + j : 9 + j, spot(s * 256 + half * 128, 128)] = fc_ref[
+                    :, start : start + 128
+                ]
+            base = place * 384
+            for i in range(2):
+                tile = mixed_ref[:, base + i * 128 : base + (i + 1) * 128]
+                query = tile[:, :DH]
+                value = mixed_ref[:, base + 256 + i * DH : base + 256 + (i + 1) * DH]
+                where = spot((2 * half + i) * 256 + (s >> 1) * 128, 128)
+                empty = jnp.zeros((1, DH), F32)
+                odd = (s & 1) == 1
+                for row, vector in ((6, query), (7, value)):
+                    held[index, row : row + 1, where] = jnp.where(
+                        odd,
+                        jnp.concatenate([empty, vector], axis=1),
+                        jnp.concatenate([vector, empty], axis=1),
+                    )
+    keep_ref[...] = held[c]
+    send_ref[...] = held[1 - c]
+
+
+def sum_kernel(ids, *refs):
+    refs[-1][...] = summed(refs[:-1])
+
+
+def final_kernel(ids, own_ref, oth_ref, po_own_ref, po_oth_ref, *refs):
+    rows = refs[:4]
+    mixed_out, fc_out, proj_out, out_out, vec_out, bfc_out = refs[4:10]
+    s, z, c = ids[0], ids[1], ids[2]
+    width = out_out.shape[2]
+    for ref, po_ref, half in ((own_ref, po_own_ref, c), (oth_ref, po_oth_ref, 1 - c)):
+        for source in range(GROUP):
+            for j in range(GROUP):
+                start = source * 512 + j * 128
+                fc_out[0, :, spot(j * 1024 + source * 256 + half * 128, 128)] = ref[
+                    :, start : start + 128
+                ].astype(F32)
+        for pair in range(2):
+            for i in range(2):
+                tiles = []
+                for source in (2 * pair, 2 * pair + 1):
+                    base = 2048 + source * 384
+                    qk = ref[:, base + i * 128 : base + (i + 1) * 128].astype(F32)
+                    v = ref[:, base + 256 + i * DH : base + 256 + (i + 1) * DH].astype(F32)
+                    tiles.append((qk[:, :DH], qk[:, DH:], v))
+                for t in range(3):
+                    start = t * width + (2 * half + i) * 256 + pair * 128
+                    mixed_out[0, :, spot(start, 128)] = jnp.concatenate(
+                        [tiles[0][t], tiles[1][t]], axis=1
+                    )
+        proj_out[0, spot(half * 128, 128), 0:512] = po_ref[0:128, :].astype(F32)
+        proj_out[0, spot(half * 128, 128), 512:1024] = po_ref[128:256, :].astype(F32)
+        out_out[0, :, spot(half * 512, 512)] = po_ref[256:320, :].astype(F32)
+    total = summed(rows)
+    vec_out[...] = total
+    bfc_out[...] = total
+
+
+def fast_body(
+    inputs,
+    cotangent,
+    segment_ids,
+    ln1_gain,
+    ln1_bias,
+    w_qkv,
+    b_query,
+    b_value,
+    w_out,
+    b_out,
+    ln2_gain,
+    ln2_bias,
+    w_fc,
+    b_fc,
+    w_proj,
+    b_proj,
+):
+    s, z, c = lax.axis_index("seq"), lax.axis_index("fsdp"), lax.axis_index("section")
+    first = c == 0
+    ids = jnp.stack([s, z, c]).astype(jnp.int32)
+    micro, tok, width = inputs.shape
+    count = segment_ids.shape[1]
+    tall = GROUP * tok
+
+    q_mine, q_send = call(
+        pick_mixed_kernel,
+        "pick_mixed",
+        ids,
+        [w_qkv],
+        [((256, 384), BF)] * 2,
+        [pltpu.VMEM((3, GROUP, 256, 128), BF), pltpu.SemaphoreType.DMA((12,))],
+        anywhere=(0,),
+    )
+    q_got = swap(q_send)
+    q_half = [jnp.where(first, q_mine, q_got), jnp.where(first, q_got, q_mine)]
+
+    def both(block):
+        own = gather(block, "fsdp")
+        return own, [swap(piece) for piece in own]
+
+    vectors = jnp.concatenate(
+        [ln1_gain, ln1_bias, b_query, b_value, b_out, ln2_gain, ln2_bias, b_proj]
+        + [lax.dynamic_slice(b_fc, (0, s * 256), (1, 256))],
+        axis=0,
+    )
+    vectors = lax.all_gather(vectors, ("section", "fsdp"), axis=0)
+    vectors = vectors.reshape(2, GROUP, 9, 256).transpose(0, 2, 1, 3).reshape(2, 9, width)
+    vectors = vectors.astype(F32)
+    vec = [vectors[0], vectors[1]]
+
+    a_mine, a_send, p_mine, p_send = call(
+        pick_rest_kernel,
+        "pick_rest",
+        ids,
+        [w_fc, w_proj, w_out],
+        [((320, 512), BF)] * 2 + [((128, 1024), BF)] * 2,
+        [pltpu.SemaphoreType.DMA((12,))],
+        anywhere=(0, 1, 2),
+    )
+    a_got, p_got = swap(a_send), swap(p_send)
+    a_half = [jnp.where(first, a_mine, a_got), jnp.where(first, a_got, a_mine)]
+    p_half = [jnp.where(first, p_mine, p_got), jnp.where(first, p_got, p_mine)]
+
+    my_segs = lax.dynamic_index_in_dim(segment_ids, c, 0, keepdims=False)
+    seg_col, seg_row = my_segs.reshape(count, 1), my_segs.reshape(1, count)
+
+    w_mixed = [both(q_half[0]), None]
+    feed_own = [lax.all_gather(a_half[0], "fsdp", axis=0), None]
+    back_own = [lax.all_gather(p_half[0], "fsdp", axis=0), None]
+    w_mixed[1] = both(q_half[1])
+    feed_own[1] = lax.all_gather(a_half[1], "fsdp", axis=0)
+    back_own[1] = lax.all_gather(p_half[1], "fsdp", axis=0)
+    feed_w = [[w, swap(w)] for w in feed_own]
+    back_w = [[w, swap(w)] for w in back_own]
+
+    x = lax.dynamic_index_in_dim(inputs, c, 0, keepdims=False)
+    piece = ((384, 128), BF)
+    small = ((128, 128), BF)
+    part = ((tok, width), BF)
+    kept = []
+    top = None
+    for layer in range(2):
+        own, oth = w_mixed[layer]
+        *packed, normed = call(
+            mixed_kernel,
+            "mixed",
+            ids,
+            gather(x, "seq") + own + oth + [vec[layer]],
+            [piece] * 4 + [((tall, width), BF)],
+            [pltpu.VMEM((GROUP, 384, 128), BF)],
+            cost=(2 * tall * width * 768, 0),
+        )
+        qkv = trade(packed, "fsdp")
+        heads = call(
+            attend_kernel,
+            "attend",
+            ids,
+            qkv + [seg_col, seg_row],
+            [small] * 4,
+            [pltpu.VMEM((count, 128), BF), pltpu.VMEM((count, DH), BF), pltpu.VMEM((count, DH), BF)],
+            cost=(4 * count * count * 256, 0),
+        )
+        heads = trade(heads, "fsdp")
+        *parts, att = call(
+            output_kernel,
+            "output",
+            ids,
+            heads + feed_w[layer],
+            [part] * 4 + [((tall, 256), BF)],
+            cost=(2 * tall * width * 256, 0),
+        )
+        res, n_two = call(
+            residual_kernel,
+            "residual",
+            ids,
+            trade(parts, "seq") + [x, vec[layer]],
+            [((tok, width), F32), part],
+        )
+        *parts, slope, act, n_full = call(
+            feed_kernel,
+            "feed",
+            ids,
+            gather(n_two, "seq") + feed_w[layer] + back_w[layer] + [vec[layer]],
+            [part] * 4 + [((tall, 1024), F32), ((tall, 1024), BF), ((tall, width), BF)],
+            cost=(4 * tall * width * 1024, 0),
+        )
+        top, low = call(
+            close_kernel,
+            "close",
+            ids,
+            trade(parts, "seq") + [res, vec[layer]],
+            [((tok, width), F32), part],
+        )
+        kept.append((x, normed, qkv, att, res, slope, act, n_full))
+        x = low
+
+    grad = lax.dynamic_index_in_dim(cotangent, c, 0, keepdims=False)
+    row_terms = [None, None]
+    fc_parts, mixed_parts, proj_parts = [None, None], [None, None], [None, None]
+    turned = [
+        (i * GROUP + j, j * GROUP + i) for i in range(GROUP) for j in range(GROUP)
+    ]
+    bottom = None
+    for layer in (1, 0):
+        x, normed, qkv, att, res, slope, act, n_full = kept[layer]
+        own, oth = w_mixed[layer]
+        *parts, d_pre, gb_full = call(
+            feed_back_kernel,
+            "feed_back",
+            ids,
+            gather(grad, "seq") + feed_w[layer] + back_w[layer] + [slope],
+            [part] * 4 + [((tall, 1024), BF), ((tall, width), BF)],
+            cost=(4 * tall * width * 1024, 0),
+        )
+        d_res, ga, two_rows = call(
+            norm_two_back_kernel,
+            "norm_two_back",
+            ids,
+            trade(parts, "seq") + [res, grad, vec[layer]],
+            [((tok, width), F32), part, ((8, width), F32)],
+        )
+        *d_heads, ga_full = call(
+            output_back_kernel,
+            "output_back",
+            ids,
+            gather(ga, "seq") + feed_w[layer],
+            [small] * 4 + [((tall, width), BF)],
+            cost=(2 * tall * width * 256, 0),
+        )
+        d_heads = trade(d_heads, "fsdp")
+        keep, send, fc_sums = call(
+            feed_grads_kernel,
+            "feed_grads",
+            ids,
+            [act, gb_full, n_full, d_pre, att, ga_full],
+            [((GROUP, 576, 512), BF)] * 2 + [((1, 1024), F32)],
+            cost=(4 * tall * width * 1152, 0),
+        )
+        (feed_sum,) = call(
+            add_kernel, "add", ids, [keep, swap(send)], [((GROUP, 576, 512), BF)]
+        )
+        feed_got = lax.psum_scatter(feed_sum, "fsdp", scatter_dimension=0)
+        d_pieces = call(
+            attend_back_kernel,
+            "attend_back",
+            ids,
+            qkv + d_heads + [seg_col, seg_row],
+            [piece] * 4,
+            [
+                pltpu.VMEM((count, 128), BF),
+                pltpu.VMEM((count, DH), BF),
+                pltpu.VMEM((count, DH), BF),
+                pltpu.VMEM((count, DH), F32),
+                pltpu.VMEM((count, DH), F32),
+                pltpu.VMEM((count, DH), F32),
+            ],
+            cost=(10 * count * count * 256, 0),
+        )
+        *parts, d_mixed = call(
+            mixed_back_kernel,
+            "mixed_back",
+            ids,
+            trade(d_pieces, "fsdp") + own + oth,
+            [part] * 4 + [((tall, 768), BF)],
+            [pltpu.VMEM((GROUP, 384, 128), BF)],
+            cost=(2 * tall * width * 768, 0),
+        )
+        d_in, low, one_rows = call(
+            norm_one_back_kernel,
+            "norm_one_back",
+            ids,
+            trade(parts, "seq") + [x, d_res, vec[layer]],
+            [((tok, width), F32), part, ((8, width), F32)],
+        )
+        *terms, mixed_sums = call(
+            mixed_grads_kernel,
+            "mixed_grads",
+            ids,
+            [normed, d_mixed],
+            [((256, 384), BF)] * 8 + [((1, 768), F32)],
+            [pltpu.VMEM((GROUP, 256, 384), BF)],
+            cost=(2 * tall * width * 768, 0),
+        )
+        keeps, sends = terms[:4], terms[4:]
+        sums = call(
+            add_kernel,
+            "add",
+            ids,
+            list(keeps) + [swap(block) for block in sends],
+            [((256, 384), BF)] * 4,
+        )
+        blocks = call(
+            split_mixed_kernel,
+            "split_mixed",
+            ids,
+            trade(sums, "fsdp"),
+            [((64, 384), BF)] * 4,
+            [pltpu.VMEM((256, 384), BF)],
+        )
+        mixed_parts[layer] = trade(blocks, "seq")
+        *blocks, proj_out = call(
+            split_feed_kernel,
+            "split_feed",
+            ids,
+            [feed_got],
+            [((64, 512), BF)] * 4 + [((320, 512), BF)],
+        )
+        fc_parts[layer] = trade(blocks, "seq")
+        proj_parts[layer] = lax.ppermute(proj_out, ("seq", "fsdp"), turned)
+        row_terms[layer] = (two_rows, one_rows, fc_sums, mixed_sums)
+        bottom = d_in
+        grad = low
+
+    keep, send = call(
+        rows_kernel,
+        "rows",
+        ids,
+        list(row_terms[0]) + list(row_terms[1]),
+        [((16, width), F32)] * 2,
+        [pltpu.VMEM((2, 16, width), F32)],
+    )
+    (rows,) = call(sum_kernel, "sum", ids, [keep, swap(send)], [((16, width), F32)])
+    (rows,) = call(sum_kernel, "sum", ids, gather(rows, "fsdp"), [((16, width), F32)])
+    rows = gather(rows, "seq")
+
+    packs = [
+        call(pack_kernel, "pack", ids, fc_parts[k] + mixed_parts[k], [((64, 3584), BF)])[0]
+        for k in range(2)
+    ]
+    mine, theirs = jnp.where(first, packs[0], packs[1]), jnp.where(first, packs[1], packs[0])
+    po_mine = jnp.where(first, proj_parts[0], proj_parts[1])
+    po_theirs = jnp.where(first, proj_parts[1], proj_parts[0])
+    g_mixed, g_fc, g_proj, g_out, totals, _ = call(
+        final_kernel,
+        "final",
+        ids,
+        [mine, swap(theirs), po_mine, swap(po_theirs)] + rows,
+        [
+            ((1, 64, 3 * width), F32),
+            ((1, 64, 4096), F32),
+            ((1, 256, width), F32),
+            ((1, 64, width), F32),
+            ((16, width), F32),
+            ((16, width), F32),
+        ],
+    )
+    place = (s * GROUP + z) * 64
+    mine = lax.dynamic_slice(totals, (0, place), (8, 64))
+    g_bfc = lax.dynamic_slice(totals, (8 + s, z * 256), (1, 256))
+
+    ends_mine = jnp.where(first, bottom, top)
+    ends_other = swap(jnp.where(first, top, bottom))
+    relay = jnp.where(
+        first, jnp.stack([ends_mine, ends_other]), jnp.stack([ends_other, ends_mine])
+    )[None]
+
+    def row(index):
+        return mine[index : index + 1]
+
+    return (
+        relay,
+        row(0),
+        row(1),
+        g_mixed,
+        row(6),
+        row(7),
+        g_out,
+        row(2),
+        row(3),
+        row(4),
+        g_fc,
+        g_bfc,
+        g_proj,
+        row(5),
+    )
+
+
+def plan(mesh):
+    fits = mesh.shape["section"] == 2 and mesh.shape["seq"] == mesh.shape["fsdp"] == GROUP
+    return fast_body if fits else body
+
+
 def solution(mesh):
     placed = (
         P(None, ("seq", "fsdp"), None),
@@ -407,7 +1297,7 @@
         P("section", "fsdp"),
     )
     return jax.shard_map(
-        body,
+        plan(mesh),
         mesh=mesh,
         in_specs=placed,
         out_specs=(

time: 2000 us -> 636 us (0.32)
  waiting for transfers between devices: 1220 us -> 213 us
  matrix products: 287 us -> 0 us
  blocking collectives: 299 us -> 24.4 us
  starting transfers between devices: 46.1 us -> 197 us
  Pallas kernels: 0 us -> 142 us
  local copies, waits for them, and re-layouts: 88.8 us -> 29.4 us
  other arithmetic: 37.7 us -> 9.89 us
    reduce_scatter x10 -> x2, waiting for transfers between devices: 883 us -> 0.01 us  [fast_body(): feed_got = lax.psum_scatter(feed_sum, 'fsdp', scatter_dimension=0)]
    dot_general x57 -> x0, matrix products: 287 us -> none  [the longest x3 34.7 us: body(): jnp.einsum('cm,cf->mf', normed_two, d_pre, preferred_element_type=jnp.flo...]
    all_gather x4, waiting for transfers between devices: 307 us -> 53.3 us  [the longest x1 27.3 us: fast_body(): feed_own = [lax.all_gather(a_half[0], 'fsdp', axis=0), None]]
    ppermute x4 -> x133, starting transfers between devices: 6.23 us -> 196 us  [the longest x102 188 us: trade(): lax.ppermute(blocks[d], axis, [(i, i ^ d) for i in range(GROUP)])]
    all_gather x15 -> x1, blocking collectives: 201 us -> 24.4 us  [fast_body(): vectors = lax.all_gather(vectors, ('section', 'fsdp'), axis=0)]
    ppermute x4 -> x133, waiting for transfers between devices: 5.29 us -> 159 us  [the longest x102 146 us: trade(): lax.ppermute(blocks[d], axis, [(i, i ^ d) for i in range(GROUP)])]
    pallas_call x0 -> x44, Pallas kernels: none -> 142 us  [call(): pl.pallas_call(kernel, name=name, out_shape=[jax.ShapeDtypeStruct(shape,...]
    unnamed x1 -> x0, blocking collectives: 78.2 us -> none
  transfers between devices with their start and end apart: 28 -> 139, of which waited for: 20 -> 64; matrix products, arithmetic and copies ran while one was open for 13% -> 2% of each run, Pallas kernels for 0% -> 18%
where the time goes in v1:
time: 636 us; the launch traced here: 631 us
  waiting for transfers between devices  213 us (33%)
  starting transfers between devices  197 us (31%)
  Pallas kernels  142 us (22%)
  local copies, waits for them, and re-layouts  29.4 us (5%)
  blocking collectives  24.4 us (4%)
  between operations  15.4 us (2%)
  other arithmetic  9.89 us (2%)
    ppermute x102, starting transfers between devices, trade(): lax.ppermute(blocks[d], axis, [(i, i ^ d) for i in range(GROUP)])  188 us
    ppermute x102, waiting for transfers between devices, trade(): lax.ppermute(blocks[d], axis, [(i, i ^ d) for i in range(GROUP)])  146 us
    pallas_call x44, Pallas kernels, call(): pl.pallas_call(kernel, name=name, out_shape=[jax.ShapeDtypeStruct(shape,...  142 us
    all_gather x1, waiting for transfers between devices, fast_body(): feed_own = [lax.all_gather(a_half[0], 'fsdp', axis=0), None]  27.3 us
    all_gather x1, waiting for transfers between devices, fast_body(): back_own = [lax.all_gather(p_half[0], 'fsdp', axis=0), None]  25.9 us
    all_gather x1, blocking collectives, fast_body(): vectors = lax.all_gather(vectors, ('section', 'fsdp'), axis=0)  24.4 us
    unnamed x319, local copies, waits for them, and re-layouts  24.4 us
    ppermute x29, waiting for transfers between devices, swap(): return lax.ppermute(block, 'section', [(0, 1), (1, 0)])  13.5 us
  transfers between devices with their start and end apart: 139, of which 64 were waited for; matrix products, arithmetic and copies ran while one was open for 2% of the time, Pallas kernels for 18%

profile of v1, /device:TPU:0, one launch (start us, length us, event | category | flops | bytes accessed | tf_op | source)
XLA Modules:
  0.0 631.4 jit_solution(2597810254644061493)
XLA Ops:
  23.0 27.3 %all-gather.11.cloned.1.call-done = bf16[1280,512]{1,0:T(8,128)(2,1)} async-done(((bf16[320,512]{1,0:T(8,128)(2,1)}), bf16[1280,512]{1,0:T(8,128)(2,1)}) %all-gather.11.cloned.1.call-update) | async-done | bytes 1310736 | tf_op jit(solution)/shard_map/all_gather | solution.py:1025
  61.8 3.9 collective-permute-done.6.refs_7_
  65.6 25.9 %all-gather.13.cloned.1.call-done = bf16[512,1024]{1,0:T(8,128)(2,1)} async-done(((bf16[128,1024]{1,0:T(8,128)(2,1)}), bf16[512,1024]{1,0:T(8,128)(2,1)}) %all-gather.13.cloned.1.call-update) | async-done | bytes 1048592 | tf_op jit(solution)/shard_map/all_gather | solution.py:1026
  92.4 24.4 %all-gather.5 = bf16[8,9,256]{2,1,0:T(8,128)(2,1)S(1)} all-gather(bf16[1,9,256]{2,1,0:T(8,128)(2,1)S(1)} %bitcast.69), channel_id=2, replica_groups=mesh['section'=2,'seq'=4,'fsdp'=4] {'section','fsdp'}, dimensions={0}, use_global_device_ids=true | all-gather | bytes 41472 | tf_op jit(solution)/shard_map/all_gather | solution.py:1003
  130.6 5.0 collective-permute-done.12.refs_2_
  136.3 4.8 attend.2
  147.3 3.9 collective-permute-done.15.refs_2_
  176.7 5.4 feed.2
  182.0 4.4 collective-permute-done.34.refs_6_
  202.1 3.8 collective-permute-done.31.refs_2_
  206.6 3.9 mixed.3
  216.2 6.0 collective-permute-done.41.refs_2_
  222.9 5.0 attend.3
  262.4 5.4 feed.3
  268.5 5.2 feed_back.2
  297.9 4.7 feed_grads.3
  302.6 4.7 collective-permute-done.108.refs_1_
  308.7 4.3 add.46
  323.0 6.1 attend_back.2
  333.5 7.2 %collective-permute-done.66.refs_1_ = bf16[384,128]{1,0:T(8,128)(2,1)S(1)} collective-permute-done((bf16[384,128]{1,0:T(8,128)(2,1)}, bf16[384,128]{1,0:T(8,128)(2,1)S(1)}, u32[]{:S(2)}, u32[]{:S(2)}) %collective-permute-start.66) | collective-permute-done | bytes 98336 | tf_op jit(solution)/shard_map/ppermute | solution.py:434
  340.8 4.8 collective-permute-done.67.refs_2_
  369.3 5.2 feed_back.3
  380.5 3.8 collective-permute-done.77.refs_3_
  399.1 4.7 feed_grads.2
  403.9 4.7 collective-permute-done.94.refs_1_
  410.0 4.4 add.44
  415.2 7.2 %collective-permute-start.81 = (bf16[128,128]{1,0:T(8,128)(2,1)S(1)}, bf16[128,128]{1,0:T(8,128)(2,1)S(1)}, u32[]{:S(2)}, u32[]{:S(2)}) collective-permute-start(bf16[128,128]{1,0:T(8,128)(2,1)S(1)} %copy-done.147), channel_id=1, source_target_pairs={{0,1},{1,0},{2,3},{3,2},{4,5},{5,4},{6,7},{7,6},{8,9},{9,8},{10,11... | collective-permute-start | bytes 98312 | tf_op jit(solution)/shard_map/ppermute | solution.py:434
  430.1 6.2 attend_back.3
  465.2 20.5 %collective-permute-done.117.refs_2_ = bf16[256,384]{1,0:T(8,128)(2,1)S(1)} collective-permute-done((bf16[256,384]{1,0:T(8,128)(2,1)}, bf16[256,384]{1,0:T(8,128)(2,1)S(1)}, u32[]{:S(2)}, u32[]{:S(2)}) %collective-permute-start.117) | collective-permute-done | bytes 196640 | tf_op jit(solution)/shard_map/ppermute | solution.py:434
  496.3 7.2 %collective-permute-start.102 = (bf16[256,384]{1,0:T(8,128)(2,1)}, bf16[256,384]{1,0:T(8,128)(2,1)S(1)}, u32[]{:S(2)}, u32[]{:S(2)}) collective-permute-start(bf16[256,384]{1,0:T(8,128)(2,1)} %get-tuple-element.282), channel_id=1, source_target_pairs={{0,1},{1,0},{2,3},{3,2},{4,5},{5,4},{6,7},{7,6},{8,9},{9,8},{10,11... | collective-permute-start | bytes 589832 | tf_op jit(solution)/shard_map/ppermute | solution.py:434
  556.0 40.1 %collective-permute-start.127 = (f32[16,1024]{1,0:T(8,128)}, f32[16,1024]{1,0:T(8,128)S(1)}, u32[]{:S(2)}, u32[]{:S(2)}) collective-permute-start(f32[16,1024]{1,0:T(8,128)} %sum.2.refs_0_), channel_id=1, source_target_pairs={{0,1},{1,0},{2,3},{3,2},{4,5},{5,4},{6,7},{7,6},{8,9},{9,8},{10,11... | collective-permute-start | bytes 196616 | tf_op jit(solution)/shard_map/ppermute | solution.py:434
  607.5 4.7 collective-permute-start.130
  (635 shorter events, 341.1 us)
Async XLA Ops:
  7.2 43.1 %all-gather.11.cloned.1.call-start = ((), (), s32[]{:S(2)}) async-start(), calls=%async_computation.4 | async-start | bytes 1638400 | tf_op jit(solution)/shard_map/all_gather | solution.py:1025
  14.9 76.7 %all-gather.13.cloned.1.call-start = ((), (), s32[]{:S(2)}) async-start(), calls=%async_computation.5 | async-start | bytes 1310720 | tf_op jit(solution)/shard_map/all_gather | solution.py:1026
  18.6 128.7 %all-gather.15.cloned.1.call-start = ((), (), s32[]{:S(2)}) async-start(), calls=%async_computation.6 | async-start | bytes 1638400 | tf_op jit(solution)/shard_map/all_gather | solution.py:1028
  19.3 156.7 %all-gather.17.cloned.1.call-start = ((), (), s32[]{:S(2)}) async-start(), calls=%async_computation.7 | async-start | bytes 1310720 | tf_op jit(solution)/shard_map/all_gather | solution.py:1029
  22.5 31.4 %collective-permute-start.3 = (bf16[256,384]{1,0:T(8,128)(2,1)}, bf16[256,384]{1,0:T(8,128)(2,1)S(1)}, u32[]{:S(2)}, u32[]{:S(2)}) collective-permute-start(bf16[256,384]{1,0:T(8,128)(2,1)} %get-tuple-element.176), channel_id=1, source_target_pairs={{0,16},{16,0},{1,17},{17,1},{2,18},{18,2},{3,19},{19,3},{4,20},{20... | collective-permute-start | bytes 589832 | tf_op jit(solution)/shard_map/ppermute | solution.py:443
  50.3 100.9 %collective-permute-start.18 = (bf16[4,320,512]{2,1,0:T(8,128)(2,1)}, bf16[4,320,512]{2,1,0:T(8,128)(2,1)S(1)}, u32[]{:S(2)}, u32[]{:S(2)}) collective-permute-start(bf16[4,320,512]{2,1,0:T(8,128)(2,1)} %bitcast.34), channel_id=1, source_target_pairs={{0,16},{16,0},{1,17},{17,1},{2,18},{18,2},{3,19},{19,3},{4,20},{20... | collective-permute-start | bytes 3932168 | tf_op jit(solution)/shard_map/ppermute | solution.py:443
  53.9 459.9 %reduce-scatter.5.cloned.1.call-start = ((), (), s32[]{:S(2)}) async-start(), calls=%async_computation.3 | async-start | bytes 2949120 | tf_op jit(solution)/shard_map/reduce_scatter | solution.py:1139
  56.7 60.2 %collective-permute-start.4 = (bf16[256,384]{1,0:T(8,128)(2,1)S(1)}, bf16[256,384]{1,0:T(8,128)(2,1)S(1)}, u32[]{:S(2)}, u32[]{:S(2)}) collective-permute-start(bf16[256,384]{1,0:T(8,128)(2,1)S(1)} %get-tuple-element.347.refs_4_), channel_id=1, source_target_pairs={{0,1},{1,0},{2,3},{3,2},{4,5},{5,4},{6,7},{7,6},{8,9},{9,8},{10,11... | collective-permute-start | bytes 589832 | tf_op jit(solution)/shard_map/ppermute | solution.py:434
  59.3 58.0 %collective-permute-start.5 = (bf16[256,384]{1,0:T(8,128)(2,1)S(1)}, bf16[256,384]{1,0:T(8,128)(2,1)S(1)}, u32[]{:S(2)}, u32[]{:S(2)}) collective-permute-start(bf16[256,384]{1,0:T(8,128)(2,1)S(1)} %get-tuple-element.347.refs_4_), channel_id=1, source_target_pairs={{0,2},{1,3},{2,0},{3,1},{4,6},{5,7},{6,4},{7,5},{8,10},{9,11},{10,... | collective-permute-start | bytes 589832 | tf_op jit(solution)/shard_map/ppermute | solution.py:434
  61.7 55.8 %collective-permute-start.7 = (bf16[256,384]{1,0:T(8,128)(2,1)S(1)}, bf16[256,384]{1,0:T(8,128)(2,1)S(1)}, u32[]{:S(2)}, u32[]{:S(2)}) collective-permute-start(bf16[256,384]{1,0:T(8,128)(2,1)S(1)} %get-tuple-element.347.refs_4_), channel_id=1, source_target_pairs={{0,16},{16,0},{1,17},{17,1},{2,18},{18,2},{3,19},{19,3},{4,20},{20... | collective-permute-start | bytes 589832 | tf_op jit(solution)/shard_map/ppermute | solution.py:443
  91.6 79.1 %collective-permute-start.26 = (bf16[4,128,1024]{2,1,0:T(8,128)(2,1)}, bf16[4,128,1024]{2,1,0:T(8,128)(2,1)}, u32[]{:S(2)}, u32[]{:S(2)}) collective-permute-start(bf16[4,128,1024]{2,1,0:T(8,128)(2,1)} %bitcast.44), channel_id=1, source_target_pairs={{0,16},{16,0},{1,17},{17,1},{2,18},{18,2},{3,19},{19,3},{4,20},{20... | collective-permute-start | bytes 3145736 | tf_op jit(solution)/shard_map/ppermute | solution.py:443
  147.3 85.0 %collective-permute-start.46 = (bf16[4,320,512]{2,1,0:T(8,128)(2,1)}, bf16[4,320,512]{2,1,0:T(8,128)(2,1)S(1)}, u32[]{:S(2)}, u32[]{:S(2)}) collective-permute-start(bf16[4,320,512]{2,1,0:T(8,128)(2,1)} %bitcast.39), channel_id=1, source_target_pairs={{0,16},{16,0},{1,17},{17,1},{2,18},{18,2},{3,19},{19,3},{4,20},{20... | collective-permute-start | bytes 3932168 | tf_op jit(solution)/shard_map/ppermute | solution.py:443
  176.0 80.2 %collective-permute-start.47 = (bf16[4,128,1024]{2,1,0:T(8,128)(2,1)}, bf16[4,128,1024]{2,1,0:T(8,128)(2,1)S(1)}, u32[]{:S(2)}, u32[]{:S(2)}) collective-permute-start(bf16[4,128,1024]{2,1,0:T(8,128)(2,1)} %bitcast.47), channel_id=1, source_target_pairs={{0,16},{16,0},{1,17},{17,1},{2,18},{18,2},{3,19},{19,3},{4,20},{20... | collective-permute-start | bytes 3145736 | tf_op jit(solution)/shard_map/ppermute | solution.py:443
  313.0 218.6 %reduce-scatter.3.cloned.1.call-start = ((), (), s32[]{:S(2)}) async-start(), calls=%async_computation.2 | async-start | bytes 2949120 | tf_op jit(solution)/shard_map/reduce_scatter | solution.py:1139
  329.1 16.5 %collective-permute-start.67 = (bf16[384,128]{1,0:T(8,128)(2,1)}, bf16[384,128]{1,0:T(8,128)(2,1)S(1)}, u32[]{:S(2)}, u32[]{:S(2)}) collective-permute-start(bf16[384,128]{1,0:T(8,128)(2,1)} %get-tuple-element.226), channel_id=1, source_target_pairs={{0,2},{1,3},{2,0},{3,1},{4,6},{5,7},{6,4},{7,5},{8,10},{9,11},{10,... | collective-permute-start | bytes 294920 | tf_op jit(solution)/shard_map/ppermute | solution.py:434
  438.7 16.5 %collective-permute-start.85 = (bf16[384,128]{1,0:T(8,128)(2,1)}, bf16[384,128]{1,0:T(8,128)(2,1)S(1)}, u32[]{:S(2)}, u32[]{:S(2)}) collective-permute-start(bf16[384,128]{1,0:T(8,128)(2,1)} %get-tuple-element.246), channel_id=1, source_target_pairs={{0,2},{1,3},{2,0},{3,1},{4,6},{5,7},{6,4},{7,5},{8,10},{9,11},{10,... | collective-permute-start | bytes 294920 | tf_op jit(solution)/shard_map/ppermute | solution.py:434
  444.4 20.8 %collective-permute-start.116 = (bf16[256,384]{1,0:T(8,128)(2,1)}, bf16[256,384]{1,0:T(8,128)(2,1)S(1)}, u32[]{:S(2)}, u32[]{:S(2)}) collective-permute-start(bf16[256,384]{1,0:T(8,128)(2,1)} %get-tuple-element.312), channel_id=1, source_target_pairs={{0,1},{1,0},{2,3},{3,2},{4,5},{5,4},{6,7},{7,6},{8,9},{9,8},{10,11... | collective-permute-start | bytes 589832 | tf_op jit(solution)/shard_map/ppermute | solution.py:434
  445.4 40.3 %collective-permute-start.117 = (bf16[256,384]{1,0:T(8,128)(2,1)}, bf16[256,384]{1,0:T(8,128)(2,1)S(1)}, u32[]{:S(2)}, u32[]{:S(2)}) collective-permute-start(bf16[256,384]{1,0:T(8,128)(2,1)} %get-tuple-element.313), channel_id=1, source_target_pairs={{0,2},{1,3},{2,0},{3,1},{4,6},{5,7},{6,4},{7,5},{8,10},{9,11},{10,... | collective-permute-start | bytes 589832 | tf_op jit(solution)/shard_map/ppermute | solution.py:434
  448.0 37.7 %collective-permute-start.118 = (bf16[256,384]{1,0:T(8,128)(2,1)}, bf16[256,384]{1,0:T(8,128)(2,1)S(1)}, u32[]{:S(2)}, u32[]{:S(2)}) collective-permute-start(bf16[256,384]{1,0:T(8,128)(2,1)} %get-tuple-element.314), channel_id=1, source_target_pairs={{0,3},{1,2},{2,1},{3,0},{4,7},{5,6},{6,5},{7,4},{8,11},{9,10},{10,... | collective-permute-start | bytes 589832 | tf_op jit(solution)/shard_map/ppermute | solution.py:434
  462.0 25.5 %collective-permute-start.100 = (bf16[256,384]{1,0:T(8,128)(2,1)}, bf16[256,384]{1,0:T(8,128)(2,1)S(1)}, u32[]{:S(2)}, u32[]{:S(2)}) collective-permute-start(bf16[256,384]{1,0:T(8,128)(2,1)} %get-tuple-element.279), channel_id=1, source_target_pairs={{0,16},{16,0},{1,17},{17,1},{2,18},{18,2},{3,19},{19,3},{4,20},{20... | collective-permute-start | bytes 589832 | tf_op jit(solution)/shard_map/ppermute | solution.py:443
  462.0 25.6 %collective-permute-start.101 = (bf16[256,384]{1,0:T(8,128)(2,1)}, bf16[256,384]{1,0:T(8,128)(2,1)S(1)}, u32[]{:S(2)}, u32[]{:S(2)}) collective-permute-start(bf16[256,384]{1,0:T(8,128)(2,1)} %get-tuple-element.280), channel_id=1, source_target_pairs={{0,16},{16,0},{1,17},{17,1},{2,18},{18,2},{3,19},{19,3},{4,20},{20... | collective-permute-start | bytes 589832 | tf_op jit(solution)/shard_map/ppermute | solution.py:443
  465.1 24.3 %collective-permute-start.98 = (bf16[256,384]{1,0:T(8,128)(2,1)}, bf16[256,384]{1,0:T(8,128)(2,1)S(1)}, u32[]{:S(2)}, u32[]{:S(2)}) collective-permute-start(bf16[256,384]{1,0:T(8,128)(2,1)} %get-tuple-element.277), channel_id=1, source_target_pairs={{0,16},{16,0},{1,17},{17,1},{2,18},{18,2},{3,19},{19,3},{4,20},{20... | collective-permute-start | bytes 589832 | tf_op jit(solution)/shard_map/ppermute | solution.py:443
  489.4 24.0 %collective-permute-start.87 = (bf16[64,1024]{1,0:T(8,128)(2,1)}, bf16[64,1024]{1,0:T(8,128)(2,1)S(1)}, u32[]{:S(2)}, u32[]{:S(2)}) collective-permute-start(bf16[64,1024]{1,0:T(8,128)(2,1)} %get-tuple-element.249), channel_id=1, source_target_pairs={{0,4},{4,0},{8,12},{12,8},{1,5},{5,1},{9,13},{13,9},{2,6},{6,2},{1... | collective-permute-start | bytes 393224 | tf_op jit(solution)/shard_map/ppermute | solution.py:434
  496.3 19.4 %collective-permute-start.102 = (bf16[256,384]{1,0:T(8,128)(2,1)}, bf16[256,384]{1,0:T(8,128)(2,1)S(1)}, u32[]{:S(2)}, u32[]{:S(2)}) collective-permute-start(bf16[256,384]{1,0:T(8,128)(2,1)} %get-tuple-element.282), channel_id=1, source_target_pairs={{0,1},{1,0},{2,3},{3,2},{4,5},{5,4},{6,7},{7,6},{8,9},{9,8},{10,11... | collective-permute-start | bytes 589832 | tf_op jit(solution)/shard_map/ppermute | solution.py:434
  503.7 17.2 %collective-permute-start.104 = (bf16[256,384]{1,0:T(8,128)(2,1)}, bf16[256,384]{1,0:T(8,128)(2,1)S(1)}, u32[]{:S(2)}, u32[]{:S(2)}) collective-permute-start(bf16[256,384]{1,0:T(8,128)(2,1)} %get-tuple-element.284), channel_id=1, source_target_pairs={{0,3},{1,2},{2,1},{3,0},{4,7},{5,6},{6,5},{7,4},{8,11},{9,10},{10,... | collective-permute-start | bytes 589832 | tf_op jit(solution)/shard_map/ppermute | solution.py:434
  515.7 20.3 %collective-permute-start.109 = (bf16[64,512]{1,0:T(8,128)(2,1)}, bf16[64,512]{1,0:T(8,128)(2,1)S(1)}, u32[]{:S(2)}, u32[]{:S(2)}) collective-permute-start(bf16[64,512]{1,0:T(8,128)(2,1)} %get-tuple-element.298), channel_id=1, source_target_pairs={{0,4},{4,0},{8,12},{12,8},{1,5},{5,1},{9,13},{13,9},{2,6},{6,2},{1... | collective-permute-start | bytes 196616 | tf_op jit(solution)/shard_map/ppermute | solution.py:434
  519.2 17.9 %collective-permute-start.110 = (bf16[64,512]{1,0:T(8,128)(2,1)}, bf16[64,512]{1,0:T(8,128)(2,1)S(1)}, u32[]{:S(2)}, u32[]{:S(2)}) collective-permute-start(bf16[64,512]{1,0:T(8,128)(2,1)} %get-tuple-element.299), channel_id=1, source_target_pairs={{0,8},{4,12},{8,0},{12,4},{1,9},{5,13},{9,1},{13,5},{2,10},{6,14},... | collective-permute-start | bytes 196616 | tf_op jit(solution)/shard_map/ppermute | solution.py:434
  520.9 16.5 %collective-permute-start.111 = (bf16[64,512]{1,0:T(8,128)(2,1)}, bf16[64,512]{1,0:T(8,128)(2,1)S(1)}, u32[]{:S(2)}, u32[]{:S(2)}) collective-permute-start(bf16[64,512]{1,0:T(8,128)(2,1)} %get-tuple-element.300), channel_id=1, source_target_pairs={{0,12},{4,8},{8,4},{12,0},{1,13},{5,9},{9,5},{13,1},{2,14},{6,10},... | collective-permute-start | bytes 196616 | tf_op jit(solution)/shard_map/ppermute | solution.py:434
  542.4 69.7 %collective-permute-start.93 = (f32[64,1024]{1,0:T(8,128)S(1)}, f32[64,1024]{1,0:T(8,128)S(1)}, u32[]{:S(2)}, u32[]{:S(2)}) collective-permute-start(f32[64,1024]{1,0:T(8,128)S(1)} %get-tuple-element.343), channel_id=1, source_target_pairs={{0,16},{16,0},{1,17},{17,1},{2,18},{18,2},{3,19},{19,3},{4,20},{20... | collective-permute-start | bytes 786440 | tf_op jit(solution)/shard_map/ppermute | solution.py:443
  549.4 68.2 %collective-permute-start.122 = (bf16[64,3584]{1,0:T(8,128)(2,1)S(1)}, bf16[64,3584]{1,0:T(8,128)(2,1)S(1)}, u32[]{:S(2)}, u32[]{:S(2)}) collective-permute-start(bf16[64,3584]{1,0:T(8,128)(2,1)S(1)} %get-tuple-element.336), channel_id=1, source_target_pairs={{0,16},{16,0},{1,17},{17,1},{2,18},{18,2},{3,19},{19,3},{4,20},{20... | collective-permute-start | bytes 1376264 | tf_op jit(solution)/shard_map/ppermute | solution.py:443
  550.6 66.9 %collective-permute-start.125 = (bf16[320,512]{1,0:T(8,128)(2,1)S(1)}, bf16[320,512]{1,0:T(8,128)(2,1)S(1)}, u32[]{:S(2)}, u32[]{:S(2)}) collective-permute-start(bf16[320,512]{1,0:T(8,128)(2,1)S(1)} %get-tuple-element.338), channel_id=1, source_target_pairs={{0,16},{16,0},{1,17},{17,1},{2,18},{18,2},{3,19},{19,3},{4,20},{20... | collective-permute-start | bytes 983048 | tf_op jit(solution)/shard_map/ppermute | solution.py:443
  556.0 42.9 %collective-permute-start.127 = (f32[16,1024]{1,0:T(8,128)}, f32[16,1024]{1,0:T(8,128)S(1)}, u32[]{:S(2)}, u32[]{:S(2)}) collective-permute-start(f32[16,1024]{1,0:T(8,128)} %sum.2.refs_0_), channel_id=1, source_target_pairs={{0,1},{1,0},{2,3},{3,2},{4,5},{5,4},{6,7},{7,6},{8,9},{9,8},{10,11... | collective-permute-start | bytes 196616 | tf_op jit(solution)/shard_map/ppermute | solution.py:434
  (264 other events, 3048.9 us)
Sparse Core Ops, SparseCore 0:
  14.9 35.3 all-gather.10
  52.4 39.0 all-gather.12
  93.7 33.1 all-gather.14
  128.9 30.3 all-gather.16
  313.2 52.6 reduce-scatter.4
  414.6 71.8 reduce-scatter.2

commit v2 on v0

--- a/solution.py
+++ b/solution.py
@@ -3,6 +3,8 @@
 import jax
 import jax.numpy as jnp
 from jax import lax
+from jax.experimental import pallas as pl
+from jax.experimental.pallas import tpu as pltpu
 from jax.sharding import PartitionSpec as P
 
 DH = 64
@@ -387,6 +389,1079 @@
     return (relay_ends,) + tuple((grad_part[None] for grad_part in totals))
 
 
+BF = jnp.bfloat16
+F32 = jnp.float32
+GROUP = 4
+SECTION, SEQ, FSDP = "section", "seq", "fsdp"
+
+
+def nt(left, right):
+    return lax.dot_general(left, right, (((1,), (1,)), ((), ())), preferred_element_type=F32)
+
+
+def tn(left, right):
+    return lax.dot_general(left, right, (((0,), (0,)), ((), ())), preferred_element_type=F32)
+
+
+def nn(left, right):
+    return jnp.dot(left, right, preferred_element_type=F32)
+
+
+def spot(start, size):
+    return pl.ds(pl.multiple_of(start, size), size)
+
+
+def call(kernel, ids, args, outs, scratch, anywhere, mib):
+    places = [pltpu.HBM if i in anywhere else pltpu.VMEM for i in range(len(args))]
+    args = [
+        pltpu.with_memory_space_constraint(a, pltpu.HBM) if i in anywhere else a
+        for i, a in enumerate(args)
+    ]
+    return pl.pallas_call(
+        kernel,
+        name=kernel.__name__.removesuffix("_kernel"),
+        out_shape=[jax.ShapeDtypeStruct(shape, dtype) for shape, dtype in outs],
+        in_specs=[pl.BlockSpec(memory_space=pltpu.SMEM)]
+        + [pl.BlockSpec(memory_space=place) for place in places],
+        out_specs=[pl.BlockSpec(memory_space=pltpu.VMEM)] * len(outs),
+        scratch_shapes=list(scratch),
+        compiler_params=pltpu.CompilerParams(vmem_limit_bytes=mib * 1024 * 1024),
+        cost_estimate=pl.CostEstimate(flops=0, bytes_accessed=0, transcendentals=0),
+    )(ids, *args)
+
+
+def after(value, *earlier):
+    return lax.optimization_barrier((value, earlier))[0]
+
+
+def exchange(block, axis, d):
+    return lax.ppermute(block, axis, [(i, i ^ d) for i in range(GROUP)])
+
+
+def trade(blocks, axis):
+    return [blocks[0]] + [exchange(blocks[d], axis, d) for d in range(1, GROUP)]
+
+
+def gather(block, axis):
+    return trade([block] * GROUP, axis)
+
+
+def swap(block):
+    return lax.ppermute(block, SECTION, [(0, 1), (1, 0)])
+
+
+def normed_rows(values, gain_vec, bias_vec):
+    average = jnp.mean(values, axis=-1, keepdims=True)
+    centred = values - average
+    variance = jnp.mean(centred * centred, axis=-1, keepdims=True)
+    return centred * lax.rsqrt(variance + EPSILON) * gain_vec + bias_vec
+
+
+def norm_pull(values, gain_vec, grad):
+    average = jnp.mean(values, axis=-1, keepdims=True)
+    centred = values - average
+    variance = jnp.mean(centred * centred, axis=-1, keepdims=True)
+    inverse = lax.rsqrt(variance + EPSILON)
+    unit = centred * inverse
+    scaled = grad * gain_vec
+    first = jnp.mean(scaled, axis=-1, keepdims=True)
+    second = jnp.mean(scaled * unit, axis=-1, keepdims=True)
+    pulled = inverse * (scaled - first - unit * second)
+    return (
+        pulled,
+        jnp.sum(grad * unit, axis=0, keepdims=True),
+        jnp.sum(grad, axis=0, keepdims=True),
+    )
+
+
+def pick_heads_kernel(ids, w_ref, out_ref, vec_ref, mine_ref, send_ref, held, rows_held, sem):
+    s, c = ids[0], ids[2]
+    width = w_ref.shape[2] // 3
+    copies = [pltpu.make_async_copy(w_ref.at[0, spot(s * 64, 64), :], held, sem.at[GROUP])]
+    for k in range(GROUP):
+        source = out_ref.at[0, pl.ds(pl.multiple_of(k * 64 + s * 16, 16), 16), :]
+        copies.append(pltpu.make_async_copy(source, rows_held.at[k], sem.at[k]))
+    for copy in copies:
+        copy.start()
+    for copy in copies:
+        copy.wait()
+
+    def head(t, j, k):
+        tile = held[:, spot(t * width + j * 256 + (k >> 1) * 128, 128)].astype(F32)
+        return tile[:, DH:] if k & 1 else tile[:, :DH]
+
+    foot = jnp.concatenate([vec_ref[...], jnp.zeros((16, 256), BF)], axis=1)
+    for ref, half in ((mine_ref, c), (send_ref, 1 - c)):
+        for k in range(GROUP):
+            for i in range(2):
+                j = 2 * half + i
+                pair = jnp.concatenate([head(0, j, k), head(1, j, k)], axis=1)
+                ref[k, 0:64, i * 128 : (i + 1) * 128] = pair.astype(BF)
+            pair = jnp.concatenate([head(2, 2 * half, k), head(2, 2 * half + 1, k)], axis=1)
+            ref[k, 0:64, 256:384] = pair.astype(BF)
+            for q in range(GROUP):
+                ref[k, q * 16 : (q + 1) * 16, 384:512] = rows_held[
+                    k, :, spot(half * 512 + q * 128, 128)
+                ]
+            ref[k, 64:80, :] = foot
+
+
+def pick_feed_kernel(ids, fc_ref, proj_ref, mine_ref, send_ref, sem):
+    s, c = ids[0], ids[2]
+    copies = []
+
+    def begin(source, target):
+        copy = pltpu.make_async_copy(source, target, sem.at[len(copies)])
+        copy.start()
+        copies.append(copy)
+
+    for ref, half in ((mine_ref, c), (send_ref, 1 - c)):
+        for k in range(GROUP):
+            for j in range(GROUP):
+                begin(
+                    fc_ref.at[0, spot(s * 64, 64), spot(j * 1024 + k * 256 + half * 128, 128)],
+                    ref.at[k, 0:64, j * 128 : (j + 1) * 128],
+                )
+            rows = spot(k * 256 + half * 128 + s * 32, 32)
+            begin(proj_ref.at[0, rows, 0:512], ref.at[k, 64:96, :])
+            begin(proj_ref.at[0, rows, 512:1024], ref.at[k, 96:128, :])
+    for copy in copies:
+        copy.wait()
+
+
+def settle_heads_kernel(ids, mine_ref, got_ref, x_ref, *refs):
+    first, z = ids[2] == 0, ids[1]
+    for d in range(GROUP):
+        mine, got = mine_ref[z ^ d], got_ref[z ^ d]
+        lower, upper = jnp.where(first, mine, got), jnp.where(first, got, mine)
+        refs[d][0:64, :] = lower[0:64]
+        refs[d][64:80, 0:256] = lower[64:80, 0:256]
+        refs[d][64:80, 256:512] = upper[64:80, 0:256]
+        refs[d][80:144, :] = x_ref[:, 0:512]
+        refs[d][144:208, :] = x_ref[:, 512:1024]
+        refs[GROUP][d] = upper[0:64]
+
+
+def settle_feed_kernel(ids, mine_ref, got_ref, heads_ref, *refs):
+    first, z = ids[2] == 0, ids[1]
+    for d in range(GROUP):
+        mine, got = mine_ref[z ^ d], got_ref[z ^ d]
+        refs[d][0:128, :] = jnp.where(first, mine, got)
+        refs[d][128:192, :] = heads_ref[d]
+        refs[GROUP + d][...] = jnp.where(first, got, mine)
+
+
+def first_heads_kernel(ids, *refs):
+    z = ids[1]
+    heads_ref, x_refs, vec_refs = refs[GROUP], refs[5:9], refs[9:11]
+    for d in range(GROUP):
+        block = refs[d][...]
+        x_refs[d][:, 0:512] = block[80:144]
+        x_refs[d][:, 512:1024] = block[144:208]
+        heads_ref[z ^ d] = block[0:64]
+        lanes = spot((z ^ d) * 256, 256)
+        for layer in range(2):
+            rows = block[64:80, layer * 256 : (layer + 1) * 256].astype(F32)
+            row = rows[8:9, :]
+            for k in range(1, GROUP):
+                row = jnp.where(z == k, rows[8 + k : 9 + k, :], row)
+            vec_refs[layer][0:8, lanes] = rows[0:8, :]
+            vec_refs[layer][8:9, lanes] = row
+
+
+def part_kernel(ids, *refs):
+    for d in range(GROUP):
+        refs[GROUP][ids[1] ^ d] = refs[d][0:128, :]
+        refs[GROUP + 1][ids[1] ^ d] = refs[d][128:192, :]
+
+
+def place_kernel(axis, ids, *refs):
+    for d in range(GROUP):
+        refs[GROUP][ids[axis] ^ d] = refs[d][...]
+
+
+def start_kernel(ids, seg_ref, x_ref, g_ref, seg_col, seg_row, x_out, g_out, sem):
+    c = ids[2]
+    copies = [
+        pltpu.make_async_copy(x_ref.at[c], x_out, sem.at[0]),
+        pltpu.make_async_copy(g_ref.at[c], g_out, sem.at[1]),
+    ]
+    for copy in copies:
+        copy.start()
+    numbers = jnp.where(c == 0, seg_ref[0:1, :], seg_ref[1:2, :]).astype(F32)
+    seg_row[...] = numbers
+    seg_col[...] = jnp.broadcast_to(numbers, (128, numbers.shape[1])).T[:, 0:1]
+    for copy in copies:
+        copy.wait()
+
+
+def mixed_piece(ref, level):
+    return jnp.concatenate([ref[k, level, :, 0:384] for k in range(GROUP)], axis=0)
+
+
+def head_rows(ref, s):
+    rows = []
+    for d in range(GROUP):
+        for k in range(GROUP):
+            tiles = [ref[k, s ^ d, q * 16 : (q + 1) * 16, 384:512] for q in range(GROUP)]
+            rows.append(jnp.concatenate(tiles, axis=1))
+    return jnp.concatenate(rows, axis=0)
+
+
+def hidden_piece(ref, level):
+    return jnp.concatenate([ref[k, level, 0:64, :] for k in range(GROUP)], axis=0)
+
+
+def back_share(ref):
+    rows = []
+    for j in range(GROUP):
+        for k in range(GROUP):
+            rows.append(jnp.concatenate([ref[k, j, 64:96, :], ref[k, j, 96:128, :]], axis=1))
+    return jnp.concatenate(rows, axis=0)
+
+
+def mixed_kernel(ids, *refs):
+    x_refs, own_ref, oth_ref, vec = refs[:4], refs[4], refs[5], refs[6]
+    out_refs, nf_ref, packed = refs[7:11], refs[11], refs[12]
+    s, z, c = ids[0], ids[1], ids[2]
+    gain_vec, bias_vec = vec[0:1, :], vec[1:2, :]
+    for d in range(GROUP):
+        nf_ref[d * 64 : (d + 1) * 64, :] = normed_rows(
+            x_refs[d][...].astype(F32), gain_vec, bias_vec
+        ).astype(BF)
+
+    def bias_of(row, j):
+        tile = vec[row : row + 1, spot(j * 256 + (z >> 1) * 128, 128)]
+        return jnp.where((z & 1) == 1, tile[:, DH:], tile[:, :DH])
+
+    empty = jnp.zeros((1, DH), F32)
+    for ref, half in ((own_ref, c), (oth_ref, 1 - c)):
+        total = jnp.zeros((GROUP * 64, 384), F32)
+        for k in range(GROUP):
+            total = total + nn(nf_ref[:, k * 256 : (k + 1) * 256], mixed_piece(ref, k))
+        j = 2 * half
+        row = jnp.concatenate(
+            [
+                bias_of(2, j),
+                empty,
+                bias_of(2, j + 1),
+                empty,
+                bias_of(3, j),
+                bias_of(3, j + 1),
+            ],
+            axis=1,
+        )
+        total = total + row
+        for i in range(2):
+            packed[j + i, 0:256, :] = total[:, i * 128 : (i + 1) * 128].astype(BF)
+            values = total[:, 256 + i * DH : 256 + (i + 1) * DH]
+            packed[j + i, 256:384, :] = jnp.concatenate(
+                [values[:128], values[128:]], axis=1
+            ).astype(BF)
+    for d in range(GROUP):
+        out_refs[d][...] = packed[s ^ d]
+
+
+def spread(ids, pieces, qk_ref, v_ref):
+    s, z = ids[0], ids[1]
+    for d in range(GROUP):
+        for e in range(GROUP):
+            rows = spot(((s ^ d) * GROUP + (z ^ e)) * 64, 64)
+            qk_ref[rows, :] = pieces[d][e * 64 : (e + 1) * 64, :]
+            lanes = slice(0, DH) if e < 2 else slice(DH, 128)
+            start = 256 + (e & 1) * 64
+            v_ref[rows, :] = pieces[d][start : start + 64, lanes]
+
+
+def block_scores(qk_ref, seg_col, seg_row, start, size):
+    stop = start + size
+    queries = qk_ref[start:stop, 0:DH] * jnp.asarray(DH ** (-0.5), BF)
+    scores = nt(queries, qk_ref[0:stop, DH:128])
+    q_place = lax.broadcasted_iota(jnp.int32, (size, stop), 0) + start
+    k_place = lax.broadcasted_iota(jnp.int32, (size, stop), 1)
+    q_doc, k_doc = seg_col[start:stop, :], seg_row[:, 0:stop]
+    same = (q_doc == k_doc) & (q_doc > 0.0)
+    allowed = ((k_place <= q_place) & same) | (k_place == q_place)
+    return jnp.where(allowed, scores, NEGATIVE)
+
+
+def attend_kernel(ids, *refs):
+    pieces, seg_col, seg_row = refs[:4], refs[4], refs[5]
+    out_refs, qk_out, v_out = refs[6:10], refs[10], refs[11]
+    qk_ref, v_ref, o_ref = refs[12:15]
+    s, z = ids[0], ids[1]
+    spread(ids, pieces, qk_ref, v_ref)
+    qk_out[...] = qk_ref[...]
+    v_out[...] = v_ref[...]
+    count = qk_ref.shape[0]
+    size = 256
+    for start in range(0, count, size):
+        scores = block_scores(qk_ref, seg_col, seg_row, start, size)
+        top = jnp.max(scores, axis=-1, keepdims=True)
+        grown = jnp.exp(scores - top)
+        total = jnp.sum(grown, axis=-1, keepdims=True)
+        mixed = nn(grown.astype(BF), v_ref[0 : start + size, :])
+        o_ref[start : start + size, :] = (mixed / total).astype(BF)
+    for d in range(GROUP):
+        for e in range(2):
+            left = o_ref[spot(((s ^ d) * GROUP + (z ^ e)) * 64, 64), :]
+            right = o_ref[spot(((s ^ d) * GROUP + (z ^ (e + 2))) * 64, 64), :]
+            out_refs[d][e * 64 : (e + 1) * 64, :] = jnp.concatenate([left, right], axis=1)
+
+
+def unpacked(piece):
+    return jnp.concatenate([piece[:, :DH], piece[:, DH:]], axis=0)
+
+
+def output_kernel(ids, *refs):
+    pieces, own_ref, oth_ref = refs[:4], refs[4], refs[5]
+    out_refs, att_ref = refs[6:10], refs[10]
+    s, c = ids[0], ids[2]
+    att = jnp.concatenate([unpacked(pieces[d][...]) for d in range(GROUP)], axis=1)
+    att_ref[...] = att
+    for w_ref, half in ((own_ref, c), (oth_ref, 1 - c)):
+        part = nn(att, head_rows(w_ref, s)).astype(BF)
+        for d in range(GROUP):
+            out_refs[d][:, spot(half * 512, 512)] = part[d * 64 : (d + 1) * 64, :]
+
+
+def summed(refs):
+    blocks = []
+    for ref in refs:
+        blocks += [ref[...]] if len(ref.shape) == 2 else [ref[k] for k in range(GROUP)]
+    total = blocks[0].astype(F32)
+    for block in blocks[1:]:
+        total = total + block.astype(F32)
+    return total
+
+
+def residual_kernel(ids, *refs):
+    x_ref, vec = refs[4], refs[5]
+    res_ref, n_ref = refs[6], refs[7]
+    res = x_ref[...].astype(F32) + summed(refs[:4]) + vec[4:5, :]
+    res_ref[...] = res
+    n_ref[...] = normed_rows(res, vec[5:6, :], vec[6:7, :]).astype(BF)
+
+
+ROOT = math.sqrt(2.0 / math.pi)
+
+
+def hidden_bias(vec, half):
+    return jnp.concatenate(
+        [vec[8:9, spot(j * 256 + half * 128, 128)] for j in range(GROUP)], axis=1
+    )
+
+
+def feed_forward(n_refs, shares, vec, c, nf_ref, keep):
+    for d in range(GROUP):
+        nf_ref[d * 64 : (d + 1) * 64, :] = n_refs[d][...]
+    part = jnp.zeros(nf_ref.shape, F32)
+    for place, half in ((0, c), (1, 1 - c)):
+        cols = slice(place * 512, (place + 1) * 512)
+        pre = jnp.zeros((GROUP * 64, 512), F32)
+        for d in range(GROUP):
+            pre = pre + nn(nf_ref[:, d * 256 : (d + 1) * 256], hidden_piece(shares[place], d))
+        pre = pre + hidden_bias(vec, half)
+        square = pre * pre
+        bend = jnp.tanh(ROOT * pre * (1.0 + 0.044715 * square))
+        act = (0.5 * pre * (1.0 + bend)).astype(BF)
+        slope = 0.5 * (1.0 + bend) + (0.5 * ROOT) * pre * (1.0 - bend * bend) * (
+            1.0 + (3.0 * 0.044715) * square
+        )
+        keep(cols, act, slope)
+        part = part + nn(act, back_share(shares[place]))
+    return part.astype(BF)
+
+
+def feed_backward(g_blocks, shares, slope_ref, out_refs, d_pre_ref, gf_ref):
+    for d in range(GROUP):
+        gf_ref[d * 64 : (d + 1) * 64, :] = g_blocks[d]
+    for place in range(2):
+        cols = slice(place * 512, (place + 1) * 512)
+        d_act = nt(gf_ref[...], back_share(shares[place]))
+        d_pre_ref[:, cols] = (d_act * slope_ref[:, cols]).astype(BF)
+    for d in range(GROUP):
+        part = nt(d_pre_ref[:, 0:512], hidden_piece(shares[0], d))
+        part = (part + nt(d_pre_ref[:, 512:1024], hidden_piece(shares[1], d))).astype(BF)
+        for e in range(GROUP):
+            out_refs[e][:, d * 256 : (d + 1) * 256] = part[e * 64 : (e + 1) * 64, :]
+
+
+def feed_kernel(ids, *refs):
+    slope_ref, act_ref, nf_ref = refs[11:14]
+
+    def keep(cols, act, slope):
+        act_ref[:, cols] = act
+        slope_ref[:, cols] = slope
+
+    part = feed_forward(refs[:4], refs[4:6], refs[6], ids[2], nf_ref, keep)
+    for d in range(GROUP):
+        refs[7 + d][...] = part[d * 64 : (d + 1) * 64, :]
+
+
+def feed_back_kernel(ids, *refs):
+    blocks = [ref[...] for ref in refs[:4]]
+    feed_backward(blocks, refs[4:6], refs[6], refs[7:11], refs[11], refs[12])
+
+
+def feed_turn_kernel(ids, *refs):
+    shares, vec, top_refs, outs = refs[8:10], refs[10], refs[11:15], refs[15:19]
+    act_ref, nf_ref, d_pre_ref, gf_ref, slope_ref = refs[19:24]
+
+    def keep(cols, act, slope):
+        act_ref[:, cols] = act
+        slope_ref[:, cols] = slope
+
+    part = feed_forward(refs[:4], shares, vec, ids[2], nf_ref, keep)
+    for d in range(GROUP):
+        top_refs[d][...] = part[d * 64 : (d + 1) * 64, :]
+    blocks = [ref[...] for ref in refs[4:8]]
+    feed_backward(blocks, shares, slope_ref, outs, d_pre_ref, gf_ref)
+
+
+def close_kernel(ids, *refs):
+    res_ref, vec, out_ref = refs[4:]
+    out = res_ref[...] + summed(refs[:4]) + vec[7:8, :]
+    out_ref[...] = out.astype(out_ref.dtype)
+
+
+def norm_two_back_kernel(ids, *refs):
+    res_ref, g_ref, vec = refs[4], refs[5], refs[6]
+    d_res_ref, ga_ref, rows_ref = refs[7:10]
+    grad = g_ref[...].astype(F32)
+    pulled, d_gain, d_bias = norm_pull(res_ref[...], vec[5:6, :], summed(refs[:4]))
+    d_res = grad + pulled
+    low = d_res.astype(BF)
+    d_res_ref[...] = d_res
+    ga_ref[...] = low
+    rows_ref[0:1, :] = jnp.sum(low.astype(F32), axis=0, keepdims=True)
+    rows_ref[1:2, :] = d_gain
+    rows_ref[2:3, :] = d_bias
+    rows_ref[3:4, :] = jnp.sum(grad.astype(BF).astype(F32), axis=0, keepdims=True)
+    rows_ref[4:8, :] = jnp.zeros((4, grad.shape[1]), F32)
+
+
+def output_back_kernel(ids, *refs):
+    g_refs, own_ref, oth_ref = refs[:4], refs[4], refs[5]
+    out_refs, gf_ref = refs[6:10], refs[10]
+    s, c = ids[0], ids[2]
+    for d in range(GROUP):
+        gf_ref[d * 64 : (d + 1) * 64, :] = g_refs[d][...]
+    d_att = nt(gf_ref[:, spot(c * 512, 512)], head_rows(own_ref, s))
+    d_att = d_att + nt(gf_ref[:, spot((1 - c) * 512, 512)], head_rows(oth_ref, s))
+    for d in range(GROUP):
+        cols = d_att[:, d * DH : (d + 1) * DH]
+        out_refs[d][...] = jnp.concatenate([cols[:128], cols[128:]], axis=1).astype(BF)
+
+
+def feed_grads_kernel(ids, *refs):
+    act_ref, gb_ref, nf_ref, d_pre_ref = refs[:4]
+    keep_ref, send_ref, sums_ref = refs[4:7]
+    for place, out_ref in ((0, keep_ref), (1, send_ref)):
+        cols = slice(place * 512, (place + 1) * 512)
+        d_fc = tn(nf_ref[...], d_pre_ref[:, cols]).astype(BF)
+        for k in range(GROUP):
+            out_ref[k, 0:256, :] = d_fc[k * 256 : (k + 1) * 256, :]
+        d_proj = tn(act_ref[:, cols], gb_ref[...]).astype(BF)
+        for j in range(GROUP):
+            rows = d_proj[j * 128 : (j + 1) * 128, :]
+            out_ref[j, 256:384, :] = rows[:, 0:512]
+            out_ref[j, 384:512, :] = rows[:, 512:1024]
+    sums_ref[...] = jnp.sum(d_pre_ref[...].astype(F32), axis=0, keepdims=True)
+
+
+def attend_back_kernel(ids, *refs):
+    d_pieces, qk_ref, v_ref, seg_col, seg_row = refs[0:4], refs[4], refs[5], refs[6], refs[7]
+    out_refs = refs[8:12]
+    do_ref, dq_ref, dk_ref, dv_ref = refs[12:16]
+    s, z = ids[0], ids[1]
+    for d in range(GROUP):
+        for e in range(GROUP):
+            rows = spot(((s ^ d) * GROUP + (z ^ e)) * 64, 64)
+            lanes = slice(0, DH) if e < 2 else slice(DH, 128)
+            start = (e & 1) * 64
+            do_ref[rows, :] = d_pieces[d][start : start + 64, lanes]
+    count = qk_ref.shape[0]
+    size = 256
+    for start in range(0, count, size):
+        stop = start + size
+        scores = block_scores(qk_ref, seg_col, seg_row, start, size)
+        top = jnp.max(scores, axis=-1, keepdims=True)
+        grown = jnp.exp(scores - top)
+        probs = grown * (1.0 / jnp.sum(grown, axis=-1, keepdims=True))
+        d_out = do_ref[start:stop, :]
+        d_weights = nt(d_out, v_ref[0:stop, :])
+        row_dot = jnp.sum(probs * d_weights, axis=-1, keepdims=True)
+        d_scores = (probs * (d_weights - row_dot) * DH ** (-0.5)).astype(BF)
+        dq_ref[start:stop, :] = nn(d_scores, qk_ref[0:stop, DH:128])
+        dk = tn(d_scores, qk_ref[start:stop, 0:DH])
+        dv = tn(probs.astype(BF), d_out)
+        if start:
+            dk_ref[0:start, :] += dk[0:start]
+            dv_ref[0:start, :] += dv[0:start]
+        dk_ref[start:stop, :] = dk[start:stop]
+        dv_ref[start:stop, :] = dv[start:stop]
+    for d in range(GROUP):
+        for e in range(GROUP):
+            rows = spot(((s ^ d) * GROUP + (z ^ e)) * 64, 64)
+            out_refs[d][e * 64 : (e + 1) * 64, :] = jnp.concatenate(
+                [dq_ref[rows, :], dk_ref[rows, :]], axis=1
+            ).astype(BF)
+        for e in range(2):
+            left = dv_ref[spot(((s ^ d) * GROUP + (z ^ e)) * 64, 64), :]
+            right = dv_ref[spot(((s ^ d) * GROUP + (z ^ (e + 2))) * 64, 64), :]
+            out_refs[d][256 + e * 64 : 320 + e * 64, :] = jnp.concatenate(
+                [left, right], axis=1
+            ).astype(BF)
+
+
+def mixed_back_kernel(ids, *refs):
+    pieces, own_ref, oth_ref = refs[:4], refs[4], refs[5]
+    out_refs, dm_ref, held = refs[6:10], refs[10], refs[11]
+    s, c = ids[0], ids[2]
+    for d in range(GROUP):
+        held[d] = pieces[d][...]
+    for place, half in ((0, c), (1, 1 - c)):
+        base = place * 384
+        values = []
+        for i in range(2):
+            d = (2 * half + i) ^ s
+            dm_ref[:, base + i * 128 : base + (i + 1) * 128] = held[d, 0:256, :]
+            values.append(unpacked(held[d, 256:384, :]))
+        dm_ref[:, base + 256 : base + 384] = jnp.concatenate(values, axis=1)
+    for k in range(GROUP):
+        part = nt(dm_ref[:, 0:384], mixed_piece(own_ref, k))
+        part = (part + nt(dm_ref[:, 384:768], mixed_piece(oth_ref, k))).astype(BF)
+        for d in range(GROUP):
+            out_refs[d][:, k * 256 : (k + 1) * 256] = part[d * 64 : (d + 1) * 64, :]
+
+
+def attend_grads_kernel(ids, *refs):
+    nf_ref, dm_ref, att_ref, ga_ref = refs[:4]
+    keep_ref, send_ref, sums_ref = refs[4:7]
+    s, c = ids[0], ids[2]
+    for place, out_ref, half in ((0, keep_ref, c), (1, send_ref, 1 - c)):
+        d_w = tn(nf_ref[...], dm_ref[:, place * 384 : (place + 1) * 384]).astype(BF)
+        for k in range(GROUP):
+            out_ref[k, :, 0:384] = d_w[k * 256 : (k + 1) * 256, :]
+        d_out = tn(att_ref[...], ga_ref[:, spot(half * 512, 512)]).astype(BF)
+        for d in range(GROUP):
+            for q in range(GROUP):
+                out_ref[s ^ d, q * 64 : (q + 1) * 64, 384:512] = d_out[
+                    d * 64 : (d + 1) * 64, q * 128 : (q + 1) * 128
+                ]
+    sums_ref[...] = jnp.sum(dm_ref[...].astype(F32), axis=0, keepdims=True)
+
+
+def norm_one_back_kernel(ids, *refs):
+    x_ref, d_res_ref, vec = refs[4], refs[5], refs[6]
+    d_in_ref, low_ref, rows_ref = refs[7:10]
+    pulled, d_gain, d_bias = norm_pull(x_ref[...].astype(F32), vec[0:1, :], summed(refs[:4]))
+    d_in = d_res_ref[...] + pulled
+    d_in_ref[...] = d_in
+    low_ref[...] = d_in.astype(BF)
+    rows_ref[0:1, :] = d_gain
+    rows_ref[1:2, :] = d_bias
+    rows_ref[2:8, :] = jnp.zeros((6, d_in.shape[1]), F32)
+
+
+def add_kernel(ids, left_ref, right_ref, *out_refs):
+    for d in range(GROUP):
+        k = ids[0] ^ d
+        out_refs[d][...] = (left_ref[k].astype(F32) + right_ref[k].astype(F32)).astype(BF)
+
+
+def join_kernel(ids, *refs):
+    refs[-1][...] = summed(refs[:-1]).astype(BF)
+
+
+def choose_kernel(ids, *refs):
+    upper, mine_ref, theirs_ref = refs[-3][...], refs[-2], refs[-1]
+    lower = summed(refs[:-3]).astype(BF)
+    first = ids[2] == 0
+    mine_ref[...] = jnp.where(first, lower, upper)
+    theirs_ref[...] = jnp.where(first, upper, lower)
+
+
+def split_feed_kernel(ids, own_ref, oth_ref, *refs):
+    back_out = refs[GROUP]
+    for d in range(GROUP):
+        rows = spot((ids[1] ^ d) * 64, 64)
+        refs[d][:, 0:512] = own_ref[rows, :]
+        refs[d][:, 512:1024] = oth_ref[rows, :]
+    for ref, half in ((own_ref, ids[2]), (oth_ref, 1 - ids[2])):
+        rows = spot(half * 128, 128)
+        back_out[0, rows, 0:512] = ref[256:384, :].astype(F32)
+        back_out[0, rows, 512:1024] = ref[384:512, :].astype(F32)
+
+
+def split_attend_kernel(ids, own_ref, oth_ref, *refs):
+    for d in range(GROUP):
+        rows = spot((ids[1] ^ d) * 64, 64)
+        refs[d][:, 0:384] = own_ref[rows, 0:384]
+        refs[d][:, 384:768] = oth_ref[rows, 0:384]
+    for ref, half in ((own_ref, ids[2]), (oth_ref, 1 - ids[2])):
+        for q in range(GROUP):
+            refs[GROUP][0, :, spot(half * 512 + q * 128, 128)] = ref[
+                q * 64 : (q + 1) * 64, 384:512
+            ].astype(F32)
+
+
+def rows_kernel(ids, *refs):
+    layers, keep_ref, send_ref = (refs[:4], refs[4:8]), refs[8], refs[9]
+    held = refs[10]
+    z, c = ids[1], ids[2]
+    for index, (two_ref, one_ref, fc_ref, mixed_ref) in enumerate(layers):
+        held[index] = jnp.zeros(held.shape[1:], F32)
+        held[index, 0:2, :] = one_ref[0:2, :]
+        held[index, 2:6, :] = two_ref[0:4, :]
+        for place, half in ((0, c), (1, 1 - c)):
+            for j in range(GROUP):
+                start = place * 512 + j * 128
+                held[index, 8 + j : 9 + j, spot(z * 256 + half * 128, 128)] = fc_ref[
+                    :, start : start + 128
+                ]
+            base = place * 384
+            for i in range(2):
+                tile = mixed_ref[:, base + i * 128 : base + (i + 1) * 128]
+                query = tile[:, :DH]
+                value = mixed_ref[:, base + 256 + i * DH : base + 256 + (i + 1) * DH]
+                where = spot((2 * half + i) * 256 + (z >> 1) * 128, 128)
+                empty = jnp.zeros((1, DH), F32)
+                odd = (z & 1) == 1
+                for row, vector in ((6, query), (7, value)):
+                    held[index, row : row + 1, where] = jnp.where(
+                        odd,
+                        jnp.concatenate([empty, vector], axis=1),
+                        jnp.concatenate([vector, empty], axis=1),
+                    )
+    keep_ref[...] = held[c]
+    send_ref[...] = held[1 - c]
+
+
+def sum_kernel(ids, *refs):
+    refs[-1][...] = summed(refs[:-1])
+
+
+def final_feed_kernel(ids, *refs):
+    fc_out = refs[GROUP]
+    for place, half in ((0, ids[2]), (1, 1 - ids[2])):
+        for d in range(GROUP):
+            for j in range(GROUP):
+                start = place * 512 + j * 128
+                lanes = spot(j * 1024 + (ids[1] ^ d) * 256 + half * 128, 128)
+                fc_out[0, :, lanes] = refs[d][:, start : start + 128].astype(F32)
+
+
+def final_attend_kernel(ids, *refs):
+    mixed, rows, mixed_out, bfc_out = refs[:4], refs[4:6], refs[6], refs[7]
+    vec_outs, total, held = refs[8:16], refs[16], refs[17]
+    s, z, c = ids[0], ids[1], ids[2]
+    width = mixed_out.shape[2] // 3
+    for d in range(GROUP):
+        held[z ^ d] = mixed[d][...]
+    for place, half in ((0, c), (1, 1 - c)):
+        base = place * 384
+        for pair in range(2):
+            for i in range(2):
+                tiles = []
+                for source in (2 * pair, 2 * pair + 1):
+                    qk = held[source, :, base + i * 128 : base + (i + 1) * 128].astype(F32)
+                    v = held[source, :, base + 256 + i * DH : base + 256 + (i + 1) * DH]
+                    tiles.append((qk[:, :DH], qk[:, DH:], v.astype(F32)))
+                for t in range(3):
+                    start = t * width + (2 * half + i) * 256 + pair * 128
+                    mixed_out[0, :, spot(start, 128)] = jnp.concatenate(
+                        [tiles[0][t], tiles[1][t]], axis=1
+                    )
+    total[...] = summed(rows)
+    tile = total[0:8, spot(s * 256 + (z >> 1) * 128, 128)]
+    tile = jnp.where((z & 1) == 1, tile[:, DH:], tile[:, :DH])
+    for row, ref in enumerate(vec_outs):
+        ref[...] = tile[row : row + 1, :]
+    bfc_out[...] = total[pl.ds(8 + s, 1), spot(z * 256, 256)]
+
+
+def fast_body(
+    inputs,
+    cotangent,
+    segment_ids,
+    ln1_gain,
+    ln1_bias,
+    w_qkv,
+    b_query,
+    b_value,
+    w_out,
+    b_out,
+    ln2_gain,
+    ln2_bias,
+    w_fc,
+    b_fc,
+    w_proj,
+    b_proj,
+):
+    s, z, c = lax.axis_index(SEQ), lax.axis_index(FSDP), lax.axis_index(SECTION)
+    first = c == 0
+    ids = jnp.stack([s, z, c]).astype(jnp.int32)
+    tok, width = inputs.shape[1:]
+    count = segment_ids.shape[1]
+    tall = GROUP * tok
+    piece = ((384, 128), BF)
+    small = ((128, 128), BF)
+    part = ((tok, width), BF)
+    wide = ((tall, width), BF)
+    line = ((tok, width), F32)
+    share = ((256, 512), BF)
+    feed_share = ((512, 512), BF)
+    rows_shape = ((16, width), F32)
+    done, awaited, lagging = [], [], []
+
+    def run(kernel, args, outs, *scratch, anywhere=(), mib=16, aside=False):
+        args = list(args)
+        earlier = done[-1:] + ([] if aside else list(awaited))
+        if earlier:
+            args[0] = after(args[0], *earlier)
+        if not aside:
+            awaited[:] = lagging
+            lagging.clear()
+        result = list(call(kernel, ids, args, outs, scratch, anywhere, mib))
+        done.append(result[-1])
+        return result
+
+    def beside(blocks, got, axis, *which, lag=False):
+        for d in which:
+            got[d] = exchange(after(blocks[d], done[-1]), axis, d)
+            (lagging if lag else awaited).append(got[d])
+
+    def of(kernel, axis):
+        def bound(*refs):
+            kernel(axis, *refs)
+
+        bound.__name__ = kernel.__name__
+        return bound
+
+    def shared(pieces, axis, shape, aside=False):
+        (whole,) = run(of(place_kernel, axis), pieces, [(shape, BF)], aside=aside)
+        return [whole, swap(whole)]
+
+    seg_col, seg_row, x, grad = run(
+        start_kernel,
+        [segment_ids, inputs, cotangent],
+        [((count, 1), F32), ((1, count), F32), part, part],
+        pltpu.SemaphoreType.DMA((2,)),
+        anywhere=(1, 2),
+    )
+    vectors = jnp.concatenate(
+        [ln1_gain, ln1_bias, b_query, b_value, b_out, ln2_gain, ln2_bias, b_proj]
+        + [b_fc[:, k * 256 : (k + 1) * 256] for k in range(GROUP)]
+        + [jnp.zeros((4, 256), BF)],
+        axis=0,
+    )
+    mine, send = run(
+        pick_heads_kernel,
+        [w_qkv, w_out, vectors],
+        [((GROUP, 80, 512), BF)] * 2,
+        pltpu.VMEM((64, 3 * width), BF),
+        pltpu.VMEM((GROUP, 16, width), BF),
+        pltpu.SemaphoreType.DMA((GROUP + 1,)),
+        anywhere=(0, 1),
+    )
+    *heads, upper_heads = run(
+        settle_heads_kernel,
+        [mine, swap(send), x],
+        [((208, 512), BF)] * 4 + [((GROUP, 64, 512), BF)],
+    )
+    heads = trade(heads, FSDP)
+    mine, send = run(
+        pick_feed_kernel,
+        [w_fc, w_proj],
+        [((GROUP, 128, 512), BF)] * 2,
+        pltpu.SemaphoreType.DMA((48,)),
+        anywhere=(0, 1),
+    )
+    got = swap(send)
+    heads, *rest = run(
+        first_heads_kernel,
+        heads,
+        [((GROUP, 64, 512), BF)] + [part] * 4 + [((16, width), F32)] * 2,
+    )
+    x_all, vec = rest[:4], rest[4:]
+    heads = gather(heads, SEQ)
+    grad_all = [grad] * GROUP
+    beside([grad] * GROUP, grad_all, FSDP, 1, 3)
+    rest = run(
+        settle_feed_kernel,
+        [mine, got, upper_heads],
+        [((192, 512), BF)] * 4 + [((128, 512), BF)] * 4,
+        aside=True,
+    )
+    rest, upper_feed = rest[:4], rest[4:]
+    head_w = [shared(heads, 0, (GROUP, GROUP, 64, 512)), None]
+
+    feed_w = [None, None]
+    kept = []
+    for layer in range(2):
+        *packed, normed = run(
+            mixed_kernel,
+            x_all + head_w[layer] + [vec[layer]],
+            [piece] * 4 + [wide],
+            pltpu.VMEM((GROUP, 384, 128), BF),
+        )
+        qkv = trade(packed, SEQ)
+        got = rest[:1] + [None] * 3
+        beside(rest, got, FSDP, 1, 3)
+        if layer == 1:
+            beside([grad] * GROUP, grad_all, FSDP, 2, lag=True)
+        *heads, qk_rows, v_rows = run(
+            attend_kernel,
+            qkv + [seg_col, seg_row],
+            [small] * 4 + [((count, 128), BF), ((count, DH), BF)],
+            pltpu.VMEM((count, 128), BF),
+            pltpu.VMEM((count, DH), BF),
+            pltpu.VMEM((count, DH), BF),
+        )
+        heads = trade(heads, SEQ)
+        beside(rest, got, FSDP, 2)
+        *parts, att = run(
+            output_kernel,
+            heads + head_w[layer],
+            [part] * 4 + [((tall, 256), BF)],
+        )
+        parts = trade(parts, FSDP)
+        if layer == 0:
+            feed, heads_later = run(
+                part_kernel,
+                got,
+                [((GROUP, 128, 512), BF), ((GROUP, 64, 512), BF)],
+                aside=True,
+            )
+        else:
+            (feed,) = run(
+                of(place_kernel, 1), got, [((GROUP, 128, 512), BF)], aside=True
+            )
+        feeds = [feed] * GROUP
+        beside(feeds, feeds, SEQ, 1, 2)
+        res, n_two = run(
+            residual_kernel, parts + [x, vec[layer]], [line, part]
+        )
+        n_all = gather(n_two, FSDP)
+        beside([feed] * GROUP, feeds, SEQ, 3)
+        feeds[0] = after(feeds[0], *n_all)
+        feed_w[layer] = shared(feeds, 0, (GROUP, GROUP, 128, 512))
+        kept.append((x, normed, qk_rows, v_rows, att, res))
+        if layer == 0:
+            *parts, slope, act, n_full = run(
+                feed_kernel,
+                n_all + feed_w[0] + [vec[0]],
+                [part] * 4 + [((tall, 1024), F32), ((tall, 1024), BF), wide],
+            )
+            parts = trade(parts, FSDP)
+            heads = [heads_later] * GROUP
+            beside(heads, heads, SEQ, 1, 2)
+            (x,) = run(close_kernel, parts + [res, vec[0]], [part])
+            x_all = gather(x, FSDP)
+            beside([heads_later] * GROUP, heads, SEQ, 3)
+            heads[0] = after(heads[0], *x_all)
+            head_w[1] = shared(heads, 0, (GROUP, GROUP, 64, 512))
+            rest = upper_feed
+        else:
+            turn = run(
+                feed_turn_kernel,
+                n_all + grad_all + feed_w[1] + [vec[1]],
+                [part] * 8 + [((tall, 1024), BF), wide, ((tall, 1024), BF), wide],
+                pltpu.VMEM((tall, 1024), F32),
+                mib=20,
+            )
+
+    def feed_terms(act, gb_full, n_full, d_pre):
+        keep, send, sums = run(
+            feed_grads_kernel,
+            [act, gb_full, n_full, d_pre],
+            [((GROUP, 512, 512), BF)] * 2 + [((1, 1024), F32)],
+            aside=True,
+        )
+        return keep, swap(send), sums
+
+    def attend_terms(normed, d_mixed, att, ga_full):
+        keep, send, sums = run(
+            attend_grads_kernel,
+            [normed, d_mixed, att, ga_full],
+            [((GROUP, 256, 512), BF)] * 2 + [((1, 768), F32)],
+            aside=True,
+        )
+        return keep, swap(send), sums
+
+    def total(keep, got, shape):
+        return run(add_kernel, [keep, got], [shape] * 4, aside=True)
+
+    def join(blocks, shape):
+        return run(join_kernel, blocks, [shape], aside=True)[0]
+
+    def norm_two_back(layer, parts, grad):
+        return run(
+            norm_two_back_kernel,
+            parts + [kept[layer][5], grad, vec[layer]],
+            [line, part, ((8, width), F32)],
+        )
+
+    def output_back(layer, ga_all):
+        return run(
+            output_back_kernel,
+            ga_all + head_w[layer],
+            [small] * 4 + [wide],
+        )
+
+    def attend_back(layer, d_heads):
+        return run(
+            attend_back_kernel,
+            d_heads + list(kept[layer][2:4]) + [seg_col, seg_row],
+            [piece] * 4,
+            pltpu.VMEM((count, DH), BF),
+            *[pltpu.VMEM((count, DH), F32)] * 3,
+        )
+
+    def mixed_back(layer, d_pieces):
+        return run(
+            mixed_back_kernel,
+            d_pieces + head_w[layer],
+            [part] * 4 + [((tall, 768), BF)],
+            pltpu.VMEM((GROUP, 384, 128), BF),
+        )
+
+    def norm_one_back(layer, parts, d_res):
+        return run(
+            norm_one_back_kernel,
+            parts + [kept[layer][0], d_res, vec[layer]],
+            [line, part, ((8, width), F32)],
+        )
+
+    row_terms = [None, None]
+    top_parts, parts = turn[:4], trade(turn[4:8], FSDP)
+    keep, got, fc_sums = feed_terms(turn[8], turn[11], turn[9], turn[10])
+    d_res, ga, two_rows = norm_two_back(1, parts, grad)
+    ga_all = gather(ga, FSDP)
+    terms = total(keep, got, feed_share)
+    upper_feed = list(terms)
+    beside(terms, upper_feed, SEQ, 1, 2)
+    *d_heads, ga_full = output_back(1, ga_all)
+    d_heads = trade(d_heads, SEQ)
+    tops = list(top_parts)
+    beside(top_parts, tops, FSDP, 1, 3)
+    d_pieces = trade(attend_back(1, d_heads), SEQ)
+    beside(top_parts, tops, FSDP, 2)
+    *parts, d_mixed = mixed_back(1, d_pieces)
+    parts = trade(parts, FSDP)
+    beside(terms, upper_feed, SEQ, 3)
+    keep, got, mixed_sums = attend_terms(kept[1][1], d_mixed, kept[1][4], ga_full)
+    (top,) = run(close_kernel, tops + [kept[1][5], vec[1]], [line], aside=True)
+    _, low, one_rows = norm_one_back(1, parts, d_res)
+    row_terms[1] = (two_rows, one_rows, fc_sums, mixed_sums)
+    g_all = gather(low, FSDP)
+    terms = total(keep, got, share)
+    upper_attend = list(terms)
+    beside(terms, upper_attend, SEQ, 1, 2)
+    upper_feed = join(upper_feed, feed_share)
+
+    *parts, d_pre, gb_full = run(
+        feed_back_kernel,
+        g_all + feed_w[0] + [slope],
+        [part] * 4 + [((tall, 1024), BF), wide],
+    )
+    parts = trade(parts, FSDP)
+    beside(terms, upper_attend, SEQ, 3)
+    keep, got, fc_sums = feed_terms(act, gb_full, n_full, d_pre)
+    terms = total(keep, got, feed_share)
+    lower_feed = list(terms)
+    beside(terms, lower_feed, SEQ, 1, 2, lag=True)
+    d_res, ga, two_rows = norm_two_back(0, parts, low)
+    ga_all = gather(ga, FSDP)
+    upper_attend = join(upper_attend, share)
+    beside(terms, lower_feed, SEQ, 3)
+    *d_heads, ga_full = output_back(0, ga_all)
+    d_heads = trade(d_heads, SEQ)
+    mine, theirs = run(
+        choose_kernel, lower_feed + [upper_feed], [feed_share] * 2, aside=True
+    )
+    got = swap(theirs)
+    d_pieces = trade(attend_back(0, d_heads), SEQ)
+    *blocks, g_proj = run(
+        split_feed_kernel,
+        [mine, got],
+        [((64, 1024), BF)] * 4 + [((1, 256, width), F32)],
+        aside=True,
+    )
+    fc_parts = list(blocks)
+    beside(blocks, fc_parts, FSDP, 3, 2)
+    *parts, d_mixed = mixed_back(0, d_pieces)
+    parts = trade(parts, FSDP)
+    keep, got, mixed_sums = attend_terms(kept[0][1], d_mixed, kept[0][4], ga_full)
+    lower_attend = trade(total(keep, got, share), SEQ)
+    bottom, _, one_rows = norm_one_back(0, parts, d_res)
+    row_terms[0] = (two_rows, one_rows, fc_sums, mixed_sums)
+
+    keep, send = run(
+        rows_kernel,
+        list(row_terms[0]) + list(row_terms[1]),
+        [rows_shape] * 2,
+        pltpu.VMEM((2, 16, width), F32),
+    )
+    rows_got = swap(send)
+
+    def folded(rows, axis, d):
+        return run(sum_kernel, [rows, exchange(rows, axis, d)], [rows_shape])[0]
+
+    mine, theirs = run(choose_kernel, lower_attend + [upper_attend], [share] * 2)
+    got = swap(theirs)
+    (rows,) = run(sum_kernel, [keep, rows_got], [rows_shape])
+    *blocks, g_out = run(
+        split_attend_kernel,
+        [mine, got],
+        [((64, 768), BF)] * 4 + [((1, 64, width), F32)],
+    )
+    mixed_parts = trade(blocks, FSDP)
+    fc_parts[1] = exchange(after(fc_parts[1], g_out), FSDP, 1)
+    rows = folded(rows, SEQ, 1)
+    rows = folded(rows, SEQ, 2)
+    (g_fc,) = run(final_feed_kernel, fc_parts, [((1, 64, 4096), F32)])
+    rows = folded(rows, FSDP, 1)
+    last = exchange(rows, FSDP, 2)
+    g_mixed, g_bfc, *vec_grads = run(
+        final_attend_kernel,
+        mixed_parts + [rows, last],
+        [((1, 64, 3 * width), F32), ((1, 256), F32)] + [((1, 64), F32)] * 8,
+        pltpu.VMEM((16, width), F32),
+        pltpu.VMEM((GROUP, 64, 768), BF),
+    )
+
+    ends_mine = jnp.where(first, bottom, top)
+    ends_other = swap(jnp.where(first, top, bottom))
+    relay = jnp.where(
+        first, jnp.stack([ends_mine, ends_other]), jnp.stack([ends_other, ends_mine])
+    )[None]
+
+    return (
+        relay,
+        vec_grads[0],
+        vec_grads[1],
+        g_mixed,
+        vec_grads[6],
+        vec_grads[7],
+        g_out,
+        vec_grads[2],
+        vec_grads[3],
+        vec_grads[4],
+        g_fc,
+        g_bfc,
+        g_proj,
+        vec_grads[5],
+    )
+
+
+def plan(mesh):
+    fits = mesh.shape[SECTION] == 2 and mesh.shape[SEQ] == mesh.shape[FSDP] == GROUP
+    return fast_body if fits else body
+
+
 def solution(mesh):
     placed = (
         P(None, ("seq", "fsdp"), None),
@@ -407,7 +1482,7 @@
         P("section", "fsdp"),
     )
     return jax.shard_map(
-        body,
+        plan(mesh),
         mesh=mesh,
         in_specs=placed,
         out_specs=(

time: 2000 us -> 449 us (0.22)
  waiting for transfers between devices: 1220 us -> 189 us
  blocking collectives: 299 us -> 0 us
  matrix products: 287 us -> 0 us
  starting transfers between devices: 46.1 us -> 169 us
  local copies, waits for them, and re-layouts: 88.8 us -> 2.28 us
  Pallas kernels: 0 us -> 76.9 us
  other arithmetic: 37.7 us -> 0.96 us
    reduce_scatter x10 -> x0, waiting for transfers between devices: 883 us -> none  [the longest x1 353 us: body(): lax.psum_scatter(local_grads[9], ('seq', 'fsdp'), scatter_dimension=0, ti...]
    all_gather x4 -> x0, waiting for transfers between devices: 307 us -> none  [the longest x1 144 us: fetch_params(): lax.all_gather(w_proj[0], 'fsdp', axis=0, tiled=True)]
    dot_general x57 -> x0, matrix products: 287 us -> none  [the longest x3 34.7 us: body(): jnp.einsum('cm,cf->mf', normed_two, d_pre, preferred_element_type=jnp.flo...]
    all_gather x15 -> x0, blocking collectives: 201 us -> none  [the longest x3 53.5 us: body(): lax.all_gather(head_rows[:, 2], 'fsdp', axis=0, tiled=True)]
    ppermute x4 -> x126, waiting for transfers between devices: 5.29 us -> 189 us  [the longest x112 173 us: exchange(): return lax.ppermute(block, axis, [(i, i ^ d) for i in range(GROUP)])]
    ppermute x4 -> x126, starting transfers between devices: 6.23 us -> 169 us  [the longest x112 167 us: exchange(): return lax.ppermute(block, axis, [(i, i ^ d) for i in range(GROUP)])]
    unnamed x1 -> x0, blocking collectives: 78.2 us -> none
    pallas_call x0 -> x56, Pallas kernels: none -> 76.9 us  [call(): pl.pallas_call(kernel, name=kernel.__name__.removesuffix('_kernel'), out_...]
  transfers between devices with their start and end apart: 28 -> 126, of which waited for: 20 -> 60; matrix products, arithmetic and copies ran while one was open for 13% -> 0% of each run, Pallas kernels for 0% -> 6%
where the time goes in v2:
time: 449 us; the launch traced here: 440 us
  waiting for transfers between devices  189 us (42%)
  starting transfers between devices  169 us (38%)
  Pallas kernels  76.9 us (17%)
    ppermute x112, waiting for transfers between devices, exchange(): return lax.ppermute(block, axis, [(i, i ^ d) for i in range(GROUP)])  173 us
    ppermute x112, starting transfers between devices, exchange(): return lax.ppermute(block, axis, [(i, i ^ d) for i in range(GROUP)])  167 us
    pallas_call x56, Pallas kernels, call(): pl.pallas_call(kernel, name=kernel.__name__.removesuffix('_kernel'), out_...  76.9 us
    ppermute x14, waiting for transfers between devices, swap(): return lax.ppermute(block, SECTION, [(0, 1), (1, 0)])  16 us
  transfers between devices with their start and end apart: 126, of which 60 were waited for; matrix products, arithmetic and copies ran while one was open for 0% of the time, Pallas kernels for 6%

profile of v2, /device:TPU:0, one launch (start us, length us, event | category | flops | bytes accessed | tf_op | source)
XLA Modules:
  0.0 439.8 jit_solution(10744495421943304191)
XLA Ops:
  16.7 7.3 %collective-permute-done.1.refs_1_ = bf16[208,512]{1,0:T(8,128)(2,1)S(1)} collective-permute-done((bf16[208,512]{1,0:T(8,128)(2,1)S(1)}, bf16[208,512]{1,0:T(8,128)(2,1)S(1)}, u32[]{:S(2)}, u32[]{:S(2)}) %collective-permute-start.1) | collective-permute-done | bytes 213024 | tf_op jit(solution)/shard_map/ppermute | solution.py:438
  24.0 8.3 %collective-permute-done.2.refs_2_ = bf16[208,512]{1,0:T(8,128)(2,1)S(1)} collective-permute-done((bf16[208,512]{1,0:T(8,128)(2,1)S(1)}, bf16[208,512]{1,0:T(8,128)(2,1)S(1)}, u32[]{:S(2)}, u32[]{:S(2)}) %collective-permute-start.2) | collective-permute-done | bytes 213024 | tf_op jit(solution)/shard_map/ppermute | solution.py:438
  51.4 5.0 %collective-permute-start.11 = (bf16[192,512]{1,0:T(8,128)(2,1)S(1)}, bf16[192,512]{1,0:T(8,128)(2,1)S(1)}, u32[]{:S(2)}, u32[]{:S(2)}) collective-permute-start(bf16[192,512]{1,0:T(8,128)(2,1)S(1)} %get-tuple-element.313), channel_id=1, source_target_pairs={{0,1},{1,0},{2,3},{3,2},{4,5},{5,4},{6,7},{7,6},{8,9},{9,8},{10,11... | collective-permute-start | bytes 589832 | tf_op jit(solution)/shard_map/ppermute | solution.py:438
  62.4 5.6 %collective-permute-done.12.refs_3_ = bf16[192,512]{1,0:T(8,128)(2,1)S(1)} collective-permute-done((bf16[192,512]{1,0:T(8,128)(2,1)S(1)}, bf16[192,512]{1,0:T(8,128)(2,1)S(1)}, u32[]{:S(2)}, u32[]{:S(2)}) %collective-permute-start.12) | collective-permute-done | bytes 196640 | tf_op jit(solution)/shard_map/ppermute | solution.py:438
  68.0 3.5 attend.2
  75.7 5.8 %collective-permute-done.16.refs_2_ = bf16[192,512]{1,0:T(8,128)(2,1)S(1)} collective-permute-done((bf16[192,512]{1,0:T(8,128)(2,1)S(1)}, bf16[192,512]{1,0:T(8,128)(2,1)S(1)}, u32[]{:S(2)}, u32[]{:S(2)}) %collective-permute-start.16) | collective-permute-done | bytes 196640 | tf_op jit(solution)/shard_map/ppermute | solution.py:438
  89.8 7.2 %collective-permute-done.21.refs_3_ = bf16[4,128,512]{2,1,0:T(8,128)(2,1)S(1)} collective-permute-done((bf16[4,128,512]{2,1,0:T(8,128)(2,1)S(1)}, bf16[4,128,512]{2,1,0:T(8,128)(2,1)S(1)}, u32[]{:S(2)}, u32[]{:S(2)}) %collective-permute-start.21) | collective-permute-done | bytes 524320 | tf_op jit(solution)/shard_map/ppermute | solution.py:438
  105.0 3.8 collective-permute-done.27.refs_3_
  108.8 5.0 %collective-permute-done.26.refs_2_ = bf16[64,1024]{1,0:T(8,128)(2,1)S(1)} collective-permute-done((bf16[64,1024]{1,0:T(8,128)(2,1)S(1)}, bf16[64,1024]{1,0:T(8,128)(2,1)S(1)}, u32[]{:S(2)}, u32[]{:S(2)}) %collective-permute-start.26) | collective-permute-done | bytes 131104 | tf_op jit(solution)/shard_map/ppermute | solution.py:438
  114.6 4.1 collective-permute-done.29.refs_5_
  130.6 5.9 %collective-permute-done.33.refs_2_ = bf16[64,1024]{1,0:T(8,128)(2,1)S(1)} collective-permute-done((bf16[64,1024]{1,0:T(8,128)(2,1)S(1)}, bf16[64,1024]{1,0:T(8,128)(2,1)S(1)}, u32[]{:S(2)}, u32[]{:S(2)}) %collective-permute-start.33) | collective-permute-done | bytes 131104 | tf_op jit(solution)/shard_map/ppermute | solution.py:438
  142.9 3.8 collective-permute-done.37.refs_3_
  146.7 4.1 collective-permute-done.36.refs_2_
  166.4 3.8 attend.3
  188.4 4.7 %collective-permute-done.51.refs_3_ = bf16[4,128,512]{2,1,0:T(8,128)(2,1)S(1)} collective-permute-done((bf16[4,128,512]{2,1,0:T(8,128)(2,1)S(1)}, bf16[4,128,512]{2,1,0:T(8,128)(2,1)S(1)}, u32[]{:S(2)}, u32[]{:S(2)}) %collective-permute-start.51) | collective-permute-done | bytes 524320 | tf_op jit(solution)/shard_map/ppermute | solution.py:438
  203.3 4.6 %collective-permute-done.56.refs_2_ = bf16[64,1024]{1,0:T(8,128)(2,1)S(1)} collective-permute-done((bf16[64,1024]{1,0:T(8,128)(2,1)S(1)}, bf16[64,1024]{1,0:T(8,128)(2,1)S(1)}, u32[]{:S(2)}, u32[]{:S(2)}) %collective-permute-start.56) | collective-permute-done | bytes 131104 | tf_op jit(solution)/shard_map/ppermute | solution.py:438
  208.7 4.1 collective-permute-done.59.refs_9_
  212.8 3.4 feed_turn.1
  224.9 7.2 %collective-permute-done.61.refs_2_ = bf16[64,1024]{1,0:T(8,128)(2,1)S(1)} collective-permute-done((bf16[64,1024]{1,0:T(8,128)(2,1)S(1)}, bf16[64,1024]{1,0:T(8,128)(2,1)S(1)}, u32[]{:S(2)}, u32[]{:S(2)}) %collective-permute-start.61) | collective-permute-done | bytes 131104 | tf_op jit(solution)/shard_map/ppermute | solution.py:438
  237.5 3.4 collective-permute-start.67
  241.0 5.9 %collective-permute-done.65.refs_2_ = bf16[512,512]{1,0:T(8,128)(2,1)S(1)} collective-permute-done((bf16[512,512]{1,0:T(8,128)(2,1)S(1)}, bf16[512,512]{1,0:T(8,128)(2,1)S(1)}, u32[]{:S(2)}, u32[]{:S(2)}) %collective-permute-start.65) | collective-permute-done | bytes 524320 | tf_op jit(solution)/shard_map/ppermute | solution.py:438
  259.6 4.7 %attend_back.2 = (bf16[384,128]{1,0:T(8,128)(2,1)S(1)}, bf16[384,128]{1,0:T(8,128)(2,1)S(1)}, bf16[384,128]{1,0:T(8,128)(2,1)S(1)}, bf16[384,128]{1,0:T(8,128)(2,1)S(1)}) custom-call(s32[3]{0:T(128)S(1)} %pad_add_fusion.ids.refs_0_, bf16[128,128]{1,0:T(8,128)(2,1)S(1)} %get-tuple-element.418.refs_0_, bf16[128,128]{1,0:T(8,128)(2,1)S(1)} %collective-permute-done.71.refs_1_, ...), custom_call_target="tpu_custom_call" | custom-call | tf_op jit(solution)/shard_map/attend_back/pallas_call | solution.py:420
  283.3 9.3 %collective-permute-done.78.refs_3_ = bf16[512,512]{1,0:T(8,128)(2,1)S(1)} collective-permute-done((bf16[512,512]{1,0:T(8,128)(2,1)S(1)}, bf16[512,512]{1,0:T(8,128)(2,1)S(1)}, u32[]{:S(2)}, u32[]{:S(2)}) %collective-permute-start.78) | collective-permute-done | bytes 524320 | tf_op jit(solution)/shard_map/ppermute | solution.py:438
  305.2 6.0 %collective-permute-done.86.refs_2_ = bf16[64,1024]{1,0:T(8,128)(2,1)S(1)} collective-permute-done((bf16[64,1024]{1,0:T(8,128)(2,1)S(1)}, bf16[64,1024]{1,0:T(8,128)(2,1)S(1)}, u32[]{:S(2)}, u32[]{:S(2)}) %collective-permute-start.86) | collective-permute-done | bytes 131104 | tf_op jit(solution)/shard_map/ppermute | solution.py:438
  324.7 5.4 %collective-permute-done.91.refs_2_ = bf16[64,1024]{1,0:T(8,128)(2,1)S(1)} collective-permute-done((bf16[64,1024]{1,0:T(8,128)(2,1)S(1)}, bf16[64,1024]{1,0:T(8,128)(2,1)S(1)}, u32[]{:S(2)}, u32[]{:S(2)}) %collective-permute-start.91) | collective-permute-done | bytes 131104 | tf_op jit(solution)/shard_map/ppermute | solution.py:438
  339.3 8.2 %collective-permute-done.95.refs_3_ = bf16[512,512]{1,0:T(8,128)(2,1)S(1)} collective-permute-done((bf16[512,512]{1,0:T(8,128)(2,1)S(1)}, bf16[512,512]{1,0:T(8,128)(2,1)S(1)}, u32[]{:S(2)}, u32[]{:S(2)}) %collective-permute-start.95) | collective-permute-done | bytes 524320 | tf_op jit(solution)/shard_map/ppermute | solution.py:438
  350.1 5.8 %collective-permute-done.94.refs_2_ = bf16[512,512]{1,0:T(8,128)(2,1)S(1)} collective-permute-done((bf16[512,512]{1,0:T(8,128)(2,1)S(1)}, bf16[512,512]{1,0:T(8,128)(2,1)S(1)}, u32[]{:S(2)}, u32[]{:S(2)}) %collective-permute-start.94) | collective-permute-done | bytes 524320 | tf_op jit(solution)/shard_map/ppermute | solution.py:438
  364.6 4.8 %attend_back.3 = (bf16[384,128]{1,0:T(8,128)(2,1)S(1)}, bf16[384,128]{1,0:T(8,128)(2,1)S(1)}, bf16[384,128]{1,0:T(8,128)(2,1)S(1)}, bf16[384,128]{1,0:T(8,128)(2,1)S(1)}) custom-call(s32[3]{0:T(128)S(1)} %pad_add_fusion.ids.refs_0_, bf16[128,128]{1,0:T(8,128)(2,1)S(1)} %get-tuple-element.486.refs_0_, bf16[128,128]{1,0:T(8,128)(2,1)S(1)} %collective-permute-done.99.refs_1_, ...), custom_call_target="tpu_custom_call" | custom-call | tf_op jit(solution)/shard_map/attend_back/pallas_call | solution.py:420
  371.0 3.6 collective-permute-start.104
  380.2 3.8 collective-permute-done.104.refs_2_
  399.5 8.7 %collective-permute-done.110.refs_2_ = bf16[64,1024]{1,0:T(8,128)(2,1)S(1)} collective-permute-done((bf16[64,1024]{1,0:T(8,128)(2,1)}, bf16[64,1024]{1,0:T(8,128)(2,1)S(1)}, u32[]{:S(2)}, u32[]{:S(2)}) %collective-permute-start.110) | collective-permute-done | bytes 131104 | tf_op jit(solution)/shard_map/ppermute | solution.py:438
  432.4 3.4 collective-permute-done.123.refs_2_
  (284 shorter events, 267.8 us)
Async XLA Ops:
  11.0 28.0 %collective-permute-start.4 = (bf16[4,128,512]{2,1,0:T(8,128)(2,1)S(1)}, bf16[4,128,512]{2,1,0:T(8,128)(2,1)S(1)}, u32[]{:S(2)}, u32[]{:S(2)}) collective-permute-start(bf16[4,128,512]{2,1,0:T(8,128)(2,1)S(1)} %get-tuple-element.292), channel_id=1, source_target_pairs={{0,16},{16,0},{1,17},{17,1},{2,18},{18,2},{3,19},{19,3},{4,20},{20... | collective-permute-start | bytes 1572872 | tf_op jit(solution)/shard_map/ppermute | solution.py:450
  14.2 18.2 %collective-permute-start.2 = (bf16[208,512]{1,0:T(8,128)(2,1)S(1)}, bf16[208,512]{1,0:T(8,128)(2,1)S(1)}, u32[]{:S(2)}, u32[]{:S(2)}) collective-permute-start(bf16[208,512]{1,0:T(8,128)(2,1)S(1)} %get-tuple-element.295), channel_id=1, source_target_pairs={{0,2},{1,3},{2,0},{3,1},{4,6},{5,7},{6,4},{7,5},{8,10},{9,11},{10,... | collective-permute-start | bytes 638984 | tf_op jit(solution)/shard_map/ppermute | solution.py:438
  16.7 15.6 %collective-permute-start.3 = (bf16[208,512]{1,0:T(8,128)(2,1)S(1)}, bf16[208,512]{1,0:T(8,128)(2,1)S(1)}, u32[]{:S(2)}, u32[]{:S(2)}) collective-permute-start(bf16[208,512]{1,0:T(8,128)(2,1)S(1)} %get-tuple-element.296), channel_id=1, source_target_pairs={{0,3},{1,2},{2,1},{3,0},{4,7},{5,6},{6,5},{7,4},{8,11},{9,10},{10,... | collective-permute-start | bytes 638984 | tf_op jit(solution)/shard_map/ppermute | solution.py:438
  83.1 13.9 %collective-permute-start.21 = (bf16[4,128,512]{2,1,0:T(8,128)(2,1)S(1)}, bf16[4,128,512]{2,1,0:T(8,128)(2,1)S(1)}, u32[]{:S(2)}, u32[]{:S(2)}) collective-permute-start(bf16[4,128,512]{2,1,0:T(8,128)(2,1)S(1)} %get-tuple-element.343.refs_1_), channel_id=1, source_target_pairs={{0,8},{4,12},{8,0},{12,4},{1,9},{5,13},{9,1},{13,5},{2,10},{6,14},... | collective-permute-start | bytes 1572872 | tf_op jit(solution)/shard_map/ppermute | solution.py:438
  84.6 13.6 %collective-permute-start.20 = (bf16[4,128,512]{2,1,0:T(8,128)(2,1)S(1)}, bf16[4,128,512]{2,1,0:T(8,128)(2,1)S(1)}, u32[]{:S(2)}, u32[]{:S(2)}) collective-permute-start(bf16[4,128,512]{2,1,0:T(8,128)(2,1)S(1)} %get-tuple-element.343.refs_1_), channel_id=1, source_target_pairs={{0,4},{4,0},{8,12},{12,8},{1,5},{5,1},{9,13},{13,9},{2,6},{6,2},{1... | collective-permute-start | bytes 1572872 | tf_op jit(solution)/shard_map/ppermute | solution.py:438
  85.4 12.8 %collective-permute-start.22 = (bf16[64,1024]{1,0:T(8,128)(2,1)S(1)}, bf16[64,1024]{1,0:T(8,128)(2,1)S(1)}, u32[]{:S(2)}, u32[]{:S(2)}) collective-permute-start(bf16[64,1024]{1,0:T(8,128)(2,1)S(1)} %get-tuple-element.337), channel_id=1, source_target_pairs={{0,1},{1,0},{2,3},{3,2},{4,5},{5,4},{6,7},{7,6},{8,9},{9,8},{10,11... | collective-permute-start | bytes 393224 | tf_op jit(solution)/shard_map/ppermute | solution.py:438
  85.4 12.9 %collective-permute-start.23 = (bf16[64,1024]{1,0:T(8,128)(2,1)S(1)}, bf16[64,1024]{1,0:T(8,128)(2,1)S(1)}, u32[]{:S(2)}, u32[]{:S(2)}) collective-permute-start(bf16[64,1024]{1,0:T(8,128)(2,1)S(1)} %get-tuple-element.338), channel_id=1, source_target_pairs={{0,2},{1,3},{2,0},{3,1},{4,6},{5,7},{6,4},{7,5},{8,10},{9,11},{10,... | collective-permute-start | bytes 393224 | tf_op jit(solution)/shard_map/ppermute | solution.py:438
  99.1 14.7 %collective-permute-start.28 = (bf16[4,128,512]{2,1,0:T(8,128)(2,1)S(1)}, bf16[4,128,512]{2,1,0:T(8,128)(2,1)S(1)}, u32[]{:S(2)}, u32[]{:S(2)}) collective-permute-start(bf16[4,128,512]{2,1,0:T(8,128)(2,1)S(1)} %get-tuple-element.343.refs_1_), channel_id=1, source_target_pairs={{0,12},{4,8},{8,4},{12,0},{1,13},{5,9},{9,5},{13,1},{2,14},{6,10},... | collective-permute-start | bytes 1572872 | tf_op jit(solution)/shard_map/ppermute | solution.py:438
  123.4 13.1 %collective-permute-start.33 = (bf16[64,1024]{1,0:T(8,128)(2,1)S(1)}, bf16[64,1024]{1,0:T(8,128)(2,1)S(1)}, u32[]{:S(2)}, u32[]{:S(2)}) collective-permute-start(bf16[64,1024]{1,0:T(8,128)(2,1)S(1)} %get-tuple-element.350), channel_id=1, source_target_pairs={{0,2},{1,3},{2,0},{3,1},{4,6},{5,7},{6,4},{7,5},{8,10},{9,11},{10,... | collective-permute-start | bytes 393224 | tf_op jit(solution)/shard_map/ppermute | solution.py:438
  137.1 13.6 %collective-permute-start.38 = (bf16[4,64,512]{2,1,0:T(8,128)(2,1)S(1)}, bf16[4,64,512]{2,1,0:T(8,128)(2,1)S(1)}, u32[]{:S(2)}, u32[]{:S(2)}) collective-permute-start(bf16[4,64,512]{2,1,0:T(8,128)(2,1)S(1)} %get-tuple-element.355.refs_1_), channel_id=1, source_target_pairs={{0,12},{4,8},{8,4},{12,0},{1,13},{5,9},{9,5},{13,1},{2,14},{6,10},... | collective-permute-start | bytes 786440 | tf_op jit(solution)/shard_map/ppermute | solution.py:438
  162.4 14.7 %collective-permute-start.45 = (bf16[64,1024]{1,0:T(8,128)(2,1)S(1)}, bf16[64,1024]{1,0:T(8,128)(2,1)S(1)}, u32[]{:S(2)}, u32[]{:S(2)}) collective-permute-start(bf16[64,1024]{1,0:T(8,128)(2,1)S(1)} %get-tuple-element.368.refs_4_.refs_5_), channel_id=1, source_target_pairs={{0,2},{1,3},{2,0},{3,1},{4,6},{5,7},{6,4},{7,5},{8,10},{9,11},{10,... | collective-permute-start | bytes 393224 | tf_op jit(solution)/shard_map/ppermute | solution.py:438
  194.5 13.5 %collective-permute-start.58 = (bf16[4,128,512]{2,1,0:T(8,128)(2,1)S(1)}, bf16[4,128,512]{2,1,0:T(8,128)(2,1)S(1)}, u32[]{:S(2)}, u32[]{:S(2)}) collective-permute-start(bf16[4,128,512]{2,1,0:T(8,128)(2,1)S(1)} %place.8.refs_1_), channel_id=1, source_target_pairs={{0,12},{4,8},{8,4},{12,0},{1,13},{5,9},{9,5},{13,1},{2,14},{6,10},... | collective-permute-start | bytes 1572872 | tf_op jit(solution)/shard_map/ppermute | solution.py:438
  218.1 15.0 %collective-permute-start.63 = (bf16[4,512,512]{2,1,0:T(8,128)(2,1)S(1)}, bf16[4,512,512]{2,1,0:T(8,128)(2,1)S(1)}, u32[]{:S(2)}, u32[]{:S(2)}) collective-permute-start(bf16[4,512,512]{2,1,0:T(8,128)(2,1)S(1)} %get-tuple-element.405), channel_id=1, source_target_pairs={{0,16},{16,0},{1,17},{17,1},{2,18},{18,2},{3,19},{19,3},{4,20},{20... | collective-permute-start | bytes 6291464 | tf_op jit(solution)/shard_map/ppermute | solution.py:450
  219.5 12.6 %collective-permute-start.61 = (bf16[64,1024]{1,0:T(8,128)(2,1)S(1)}, bf16[64,1024]{1,0:T(8,128)(2,1)S(1)}, u32[]{:S(2)}, u32[]{:S(2)}) collective-permute-start(bf16[64,1024]{1,0:T(8,128)(2,1)S(1)} %get-tuple-element.398), channel_id=1, source_target_pairs={{0,2},{1,3},{2,0},{3,1},{4,6},{5,7},{6,4},{7,5},{8,10},{9,11},{10,... | collective-permute-start | bytes 393224 | tf_op jit(solution)/shard_map/ppermute | solution.py:438
  234.2 12.7 %collective-permute-start.65 = (bf16[512,512]{1,0:T(8,128)(2,1)S(1)}, bf16[512,512]{1,0:T(8,128)(2,1)S(1)}, u32[]{:S(2)}, u32[]{:S(2)}) collective-permute-start(bf16[512,512]{1,0:T(8,128)(2,1)S(1)} %get-tuple-element.410), channel_id=1, source_target_pairs={{0,8},{4,12},{8,0},{12,4},{1,9},{5,13},{9,1},{13,5},{2,10},{6,14},... | collective-permute-start | bytes 1572872 | tf_op jit(solution)/shard_map/ppermute | solution.py:438
  234.2 13.3 %collective-permute-start.64 = (bf16[512,512]{1,0:T(8,128)(2,1)S(1)}, bf16[512,512]{1,0:T(8,128)(2,1)S(1)}, u32[]{:S(2)}, u32[]{:S(2)}) collective-permute-start(bf16[512,512]{1,0:T(8,128)(2,1)S(1)} %get-tuple-element.408), channel_id=1, source_target_pairs={{0,4},{4,0},{8,12},{12,8},{1,5},{5,1},{9,13},{13,9},{2,6},{6,2},{1... | collective-permute-start | bytes 1572872 | tf_op jit(solution)/shard_map/ppermute | solution.py:438
  237.5 13.3 %collective-permute-start.67 = (bf16[64,1024]{1,0:T(8,128)(2,1)S(1)}, bf16[64,1024]{1,0:T(8,128)(2,1)S(1)}, u32[]{:S(2)}, u32[]{:S(2)}) collective-permute-start(bf16[64,1024]{1,0:T(8,128)(2,1)S(1)} %get-tuple-element.411.refs_0_), channel_id=1, source_target_pairs={{0,2},{1,3},{2,0},{3,1},{4,6},{5,7},{6,4},{7,5},{8,10},{9,11},{10,... | collective-permute-start | bytes 393224 | tf_op jit(solution)/shard_map/ppermute | solution.py:438
  277.3 16.9 %collective-permute-start.82 = (bf16[4,256,512]{2,1,0:T(8,128)(2,1)S(1)}, bf16[4,256,512]{2,1,0:T(8,128)(2,1)S(1)}, u32[]{:S(2)}, u32[]{:S(2)}) collective-permute-start(bf16[4,256,512]{2,1,0:T(8,128)(2,1)S(1)} %get-tuple-element.447), channel_id=1, source_target_pairs={{0,16},{16,0},{1,17},{17,1},{2,18},{18,2},{3,19},{19,3},{4,20},{20... | collective-permute-start | bytes 3145736 | tf_op jit(solution)/shard_map/ppermute | solution.py:450
  277.3 15.2 %collective-permute-start.78 = (bf16[512,512]{1,0:T(8,128)(2,1)S(1)}, bf16[512,512]{1,0:T(8,128)(2,1)S(1)}, u32[]{:S(2)}, u32[]{:S(2)}) collective-permute-start(bf16[512,512]{1,0:T(8,128)(2,1)S(1)} %get-tuple-element.436), channel_id=1, source_target_pairs={{0,12},{4,8},{8,4},{12,0},{1,13},{5,9},{9,5},{13,1},{2,14},{6,10},... | collective-permute-start | bytes 1572872 | tf_op jit(solution)/shard_map/ppermute | solution.py:438
  278.2 14.3 %collective-permute-start.79 = (bf16[64,1024]{1,0:T(8,128)(2,1)S(1)}, bf16[64,1024]{1,0:T(8,128)(2,1)S(1)}, u32[]{:S(2)}, u32[]{:S(2)}) collective-permute-start(bf16[64,1024]{1,0:T(8,128)(2,1)S(1)} %get-tuple-element.438), channel_id=1, source_target_pairs={{0,1},{1,0},{2,3},{3,2},{4,5},{5,4},{6,7},{7,6},{8,9},{9,8},{10,11... | collective-permute-start | bytes 393224 | tf_op jit(solution)/shard_map/ppermute | solution.py:438
  298.5 12.7 %collective-permute-start.86 = (bf16[64,1024]{1,0:T(8,128)(2,1)S(1)}, bf16[64,1024]{1,0:T(8,128)(2,1)S(1)}, u32[]{:S(2)}, u32[]{:S(2)}) collective-permute-start(bf16[64,1024]{1,0:T(8,128)(2,1)S(1)} %get-tuple-element.454.refs_0_.refs_5_), channel_id=1, source_target_pairs={{0,2},{1,3},{2,0},{3,1},{4,6},{5,7},{6,4},{7,5},{8,10},{9,11},{10,... | collective-permute-start | bytes 393224 | tf_op jit(solution)/shard_map/ppermute | solution.py:438
  317.2 12.9 %collective-permute-start.91 = (bf16[64,1024]{1,0:T(8,128)(2,1)S(1)}, bf16[64,1024]{1,0:T(8,128)(2,1)S(1)}, u32[]{:S(2)}, u32[]{:S(2)}) collective-permute-start(bf16[64,1024]{1,0:T(8,128)(2,1)S(1)} %get-tuple-element.469), channel_id=1, source_target_pairs={{0,2},{1,3},{2,0},{3,1},{4,6},{5,7},{6,4},{7,5},{8,10},{9,11},{10,... | collective-permute-start | bytes 393224 | tf_op jit(solution)/shard_map/ppermute | solution.py:438
  331.7 15.8 %collective-permute-start.95 = (bf16[512,512]{1,0:T(8,128)(2,1)S(1)}, bf16[512,512]{1,0:T(8,128)(2,1)S(1)}, u32[]{:S(2)}, u32[]{:S(2)}) collective-permute-start(bf16[512,512]{1,0:T(8,128)(2,1)S(1)} %get-tuple-element.479), channel_id=1, source_target_pairs={{0,12},{4,8},{8,4},{12,0},{1,13},{5,9},{9,5},{13,1},{2,14},{6,10},... | collective-permute-start | bytes 1572872 | tf_op jit(solution)/shard_map/ppermute | solution.py:438
  332.6 23.3 %collective-permute-start.94 = (bf16[512,512]{1,0:T(8,128)(2,1)S(1)}, bf16[512,512]{1,0:T(8,128)(2,1)S(1)}, u32[]{:S(2)}, u32[]{:S(2)}) collective-permute-start(bf16[512,512]{1,0:T(8,128)(2,1)S(1)} %get-tuple-element.478), channel_id=1, source_target_pairs={{0,8},{4,12},{8,0},{12,4},{1,9},{5,13},{9,1},{13,5},{2,10},{6,14},... | collective-permute-start | bytes 1572872 | tf_op jit(solution)/shard_map/ppermute | solution.py:438
  333.5 22.4 %collective-permute-start.93 = (bf16[512,512]{1,0:T(8,128)(2,1)S(1)}, bf16[512,512]{1,0:T(8,128)(2,1)S(1)}, u32[]{:S(2)}, u32[]{:S(2)}) collective-permute-start(bf16[512,512]{1,0:T(8,128)(2,1)S(1)} %get-tuple-element.476), channel_id=1, source_target_pairs={{0,4},{4,0},{8,12},{12,8},{1,5},{5,1},{9,13},{13,9},{2,6},{6,2},{1... | collective-permute-start | bytes 1572872 | tf_op jit(solution)/shard_map/ppermute | solution.py:438
  335.3 20.7 %collective-permute-start.98 = (bf16[64,1024]{1,0:T(8,128)(2,1)S(1)}, bf16[64,1024]{1,0:T(8,128)(2,1)S(1)}, u32[]{:S(2)}, u32[]{:S(2)}) collective-permute-start(bf16[64,1024]{1,0:T(8,128)(2,1)S(1)} %get-tuple-element.480.refs_0_), channel_id=1, source_target_pairs={{0,3},{1,2},{2,1},{3,0},{4,7},{5,6},{6,5},{7,4},{8,11},{9,10},{10,... | collective-permute-start | bytes 393224 | tf_op jit(solution)/shard_map/ppermute | solution.py:438
  336.7 19.2 %collective-permute-start.97 = (bf16[64,1024]{1,0:T(8,128)(2,1)S(1)}, bf16[64,1024]{1,0:T(8,128)(2,1)S(1)}, u32[]{:S(2)}, u32[]{:S(2)}) collective-permute-start(bf16[64,1024]{1,0:T(8,128)(2,1)S(1)} %get-tuple-element.480.refs_0_), channel_id=1, source_target_pairs={{0,2},{1,3},{2,0},{3,1},{4,6},{5,7},{6,4},{7,5},{8,10},{9,11},{10,... | collective-permute-start | bytes 393224 | tf_op jit(solution)/shard_map/ppermute | solution.py:438
  371.0 13.0 %collective-permute-start.104 = (bf16[64,1024]{1,0:T(8,128)(2,1)S(1)}, bf16[64,1024]{1,0:T(8,128)(2,1)S(1)}, u32[]{:S(2)}, u32[]{:S(2)}) collective-permute-start(bf16[64,1024]{1,0:T(8,128)(2,1)S(1)} %get-tuple-element.499), channel_id=1, source_target_pairs={{0,2},{1,3},{2,0},{3,1},{4,6},{5,7},{6,4},{7,5},{8,10},{9,11},{10,... | collective-permute-start | bytes 393224 | tf_op jit(solution)/shard_map/ppermute | solution.py:438
  392.2 18.2 %collective-permute-start.113 = (bf16[256,512]{1,0:T(8,128)(2,1)}, bf16[256,512]{1,0:T(8,128)(2,1)S(1)}, u32[]{:S(2)}, u32[]{:S(2)}) collective-permute-start(bf16[256,512]{1,0:T(8,128)(2,1)} %get-tuple-element.522), channel_id=1, source_target_pairs={{0,4},{4,0},{8,12},{12,8},{1,5},{5,1},{9,13},{13,9},{2,6},{6,2},{1... | collective-permute-start | bytes 786440 | tf_op jit(solution)/shard_map/ppermute | solution.py:438
  392.8 17.6 %collective-permute-start.114 = (bf16[256,512]{1,0:T(8,128)(2,1)}, bf16[256,512]{1,0:T(8,128)(2,1)S(1)}, u32[]{:S(2)}, u32[]{:S(2)}) collective-permute-start(bf16[256,512]{1,0:T(8,128)(2,1)} %get-tuple-element.523), channel_id=1, source_target_pairs={{0,8},{4,12},{8,0},{12,4},{1,9},{5,13},{9,1},{13,5},{2,10},{6,14},... | collective-permute-start | bytes 786440 | tf_op jit(solution)/shard_map/ppermute | solution.py:438
  394.0 16.5 %collective-permute-start.115 = (bf16[256,512]{1,0:T(8,128)(2,1)S(1)}, bf16[256,512]{1,0:T(8,128)(2,1)S(1)}, u32[]{:S(2)}, u32[]{:S(2)}) collective-permute-start(bf16[256,512]{1,0:T(8,128)(2,1)S(1)} %get-tuple-element.510), channel_id=1, source_target_pairs={{0,12},{4,8},{8,4},{12,0},{1,13},{5,9},{9,5},{13,1},{2,14},{6,10},... | collective-permute-start | bytes 786440 | tf_op jit(solution)/shard_map/ppermute | solution.py:438
  411.8 19.7 %collective-permute-start.112 = (f32[64,1024]{1,0:T(8,128)S(1)}, f32[64,1024]{1,0:T(8,128)S(1)}, u32[]{:S(2)}, u32[]{:S(2)}) collective-permute-start(f32[64,1024]{1,0:T(8,128)S(1)} %get-tuple-element.553), channel_id=1, source_target_pairs={{0,16},{16,0},{1,17},{17,1},{2,18},{18,2},{3,19},{19,3},{4,20},{20... | collective-permute-start | bytes 786440 | tf_op jit(solution)/shard_map/ppermute | solution.py:450
  (95 other events, 738.8 us)
